TPU v7x, 32 devices: a whole 2x2x4 slice. The times are simulated.
32 devices in a mesh: expert: 16 (over z, y, x), fsdp: 2 (over core).
Axes of the slice: x: 2, y: 2, z: 4, core: 2. Of those that a mesh axis runs over, the one named last changes fastest.
Arguments:
- tokens: bfloat16 [4096, 768], P(('expert', 'fsdp')), may hold values from -12 to 12
- cotangent: bfloat16 [4096, 768], P(('expert', 'fsdp')), may hold values from -6 to 6
- qkv_weight: bfloat16 [768, 2304], P('fsdp'), may hold values from -0.21875 to 0.21875
- qkv_moment: float32 [32, 55296], P(('expert', 'fsdp')), may hold values from -40 to 40
- qkv_square: float32 [32, 55296], P(('expert', 'fsdp')), may hold values from 4.096 to 16.384
- out_weight: bfloat16 [768, 768], P('fsdp'), may hold values from -1.75 to 1.75
- out_moment: float32 [32, 18432], P(('expert', 'fsdp')), may hold values from -4 to 4
- out_square: float32 [32, 18432], P(('expert', 'fsdp')), may hold values from 0.04096 to 0.16384
- up_experts: bfloat16 [16, 768, 1536], P('expert', None, 'fsdp'), may hold values from -0.21875 to 0.21875
- up_moment: float32 [16, 768, 1536], P('expert', None, 'fsdp'), may hold values from -6 to 6
- up_square: float32 [16, 768, 1536], P('expert', None, 'fsdp'), may hold values from 0.08192 to 0.3328
- down_experts: bfloat16 [16, 1536, 768], P('expert', 'fsdp'), may hold values from -1.25 to 1.25
- down_moment: float32 [16, 1536, 768], P('expert', 'fsdp'), may hold values from -1.25 to 1.25
- down_square: float32 [16, 1536, 768], P('expert', 'fsdp'), may hold values from 0.0034 to 0.0136
- router_weight: bfloat16 [768, 8], replicated, may hold values from -0.109375 to 0.109375
- router_moment: float32 [768, 8], replicated, may hold values from -448 to 448
- router_square: float32 [768, 8], replicated, may hold values from 393.216 to 1572.864
- norm_gains: bfloat16 [2, 768], replicated, may hold values from 0.5 to 1.5
- gain_moment: float32 [2, 768], replicated, may hold values from -40 to 40
- gain_square: float32 [2, 768], replicated, may hold values from 4.096 to 16.384
- relative_position_bias: bfloat16 [32, 12], replicated, may hold values from -6 to 6
- bias_moment: float32 [32, 12], replicated, may hold values from -128 to 128
- bias_square: float32 [32, 12], replicated, may hold values from 41.94304 to 167.77216
- expert_ids: int32 [4096], P(('expert', 'fsdp')), may hold values from 0 to 7, as said below
- slot_ids: int32 [4096], P(('expert', 'fsdp')), may hold values from -1 to 19, as said below
Outputs:
- block_out: bfloat16 [4096, 768], P(('expert', 'fsdp'))
- tokens_grad: float32 [4096, 768], P(('expert', 'fsdp'))
- new_qkv_moment: float32 [32, 55296], P(('expert', 'fsdp'))
- new_qkv_square: float32 [32, 55296], P(('expert', 'fsdp'))
- new_qkv_weight: float32 [32, 55296], P(('expert', 'fsdp'))
- new_out_moment: float32 [32, 18432], P(('expert', 'fsdp'))
- new_out_square: float32 [32, 18432], P(('expert', 'fsdp'))
- new_out_weight: float32 [32, 18432], P(('expert', 'fsdp'))
- new_up_moment: float32 [16, 768, 1536], P('expert', None, 'fsdp')
- new_up_square: float32 [16, 768, 1536], P('expert', None, 'fsdp')
- new_up_experts: float32 [16, 768, 1536], P('expert', None, 'fsdp')
- new_down_moment: float32 [16, 1536, 768], P('expert', 'fsdp')
- new_down_square: float32 [16, 1536, 768], P('expert', 'fsdp')
- new_down_experts: float32 [16, 1536, 768], P('expert', 'fsdp')
- new_router_moment: float32 [768, 8], replicated
- new_router_square: float32 [768, 8], replicated
- new_router_weight: float32 [768, 8], replicated
- new_gain_moment: float32 [2, 768], replicated
- new_gain_square: float32 [2, 768], replicated
- new_gains: float32 [2, 768], replicated
- new_bias_moment: float32 [32, 12], replicated
- new_bias_square: float32 [32, 12], replicated
- new_rel_bias: float32 [32, 12], replicated
Inputs may be any that keep to these rules, and one draw needn't show every extreme that they name: `expert_ids`: every expert is chosen by some token of the first device. `slot_ids`: for each token, the number of earlier tokens of the same device with the same expert, or -1 where that number is 20 or more. On every device some expert fills all 20 slots.
All inputs are finite; a program needn't handle non-finite values.
Results may differ from a plain program's by a relative error of at most 0.014.
Values may be sent and summed in bfloat16 or wider, within the bound.
A program may use at most 128 MiB of HBM per device.

v0:
```python
import jax
import jax.numpy as jnp
from jax import lax
from jax.sharding import PartitionSpec as P

FF = 3072
STEP = 10


EPS_NORM = 1e-06
BETA_ONE = 0.9
BETA_TWO = 0.999
ADAM_EPS = 1e-08
DECAY = 0.1
ROOT_HALF = 0.7071067811865476
INV_ROOT_TWO_PI = 0.3989422804014327


def norm_forward(value, gain):
    inverse = lax.rsqrt(jnp.mean(value * value, axis=-1, keepdims=True) + EPS_NORM)
    return (value * inverse * gain, inverse)


def norm_backward(value, inverse, gain, upstream):
    scaled = upstream * gain
    normal = value * inverse
    gain_grad = jnp.sum(normal * upstream, axis=0)
    value_grad = inverse * (scaled - normal * jnp.mean(normal * scaled, axis=-1, keepdims=True))
    return (value_grad, gain_grad)


def gelu_value(value):
    return 0.5 * value * (1.0 + lax.erf(value * ROOT_HALF))


def gelu_derivative(value):
    return (
        0.5 * (1.0 + lax.erf(value * ROOT_HALF))
        + value * jnp.exp(-0.5 * value * value) * INV_ROOT_TWO_PI
    )


def bucket_ids(query_pos, key_pos):
    relative = key_pos[None, :] - query_pos[:, None]
    distance = jnp.abs(relative)
    far_bucket = jnp.full(distance.shape, 8, jnp.int32)
    for degree in range(1, 8):
        far_bucket = far_bucket + (distance * distance >= 2 ** (degree + 6)).astype(jnp.int32)
    return jnp.where(distance < 8, distance, far_bucket) + 16 * (relative > 0).astype(jnp.int32)


def adam_step(weight, moment, square, grad, rate, decay):
    new_moment = BETA_ONE * moment + (1.0 - BETA_ONE) * grad
    new_square = BETA_TWO * square + (1.0 - BETA_TWO) * grad * grad
    moment_hat = new_moment / (1.0 - BETA_ONE**STEP)
    square_hat = new_square / (1.0 - BETA_TWO**STEP)
    new_weight = weight - rate * (moment_hat / (jnp.sqrt(square_hat) + ADAM_EPS) + decay * weight)
    return (new_moment, new_square, new_weight)


def to_experts(row_block):
    doubled = jnp.repeat(row_block, 2, axis=0)
    return lax.all_to_all(doubled, "expert", split_axis=0, concat_axis=0, tiled=True)


def from_experts(partial_rows):
    returned = lax.all_to_all(
        partial_rows.astype(jnp.bfloat16), "expert", split_axis=0, concat_axis=0, tiled=True
    ).astype(partial_rows.dtype)
    device_count, capacity, model_width = returned.shape
    return jnp.sum(returned.reshape(device_count // 2, 2, capacity, model_width), axis=1)


def all_rows(row_block):
    return lax.all_gather(row_block, "fsdp", axis=0, tiled=True)


def sum_quarters(term_fn, row_count):
    return lax.psum_scatter(
        term_fn(jnp.int32(0), row_count * lax.axis_size("fsdp")).astype(jnp.bfloat16),
        "fsdp",
        scatter_dimension=0,
        tiled=True,
    ).astype(jnp.float32)


def local(
    tokens,
    cotangent,
    qkv_weight,
    qkv_moment,
    qkv_square,
    out_weight,
    out_moment,
    out_square,
    up_experts,
    up_moment,
    up_square,
    down_experts,
    down_moment,
    down_square,
    router_weight,
    router_moment,
    router_square,
    norm_gains,
    gain_moment,
    gain_square,
    relative_position_bias,
    bias_moment,
    bias_square,
    expert_ids,
    slot_ids,
):
    tok_rows, model_width = tokens.shape
    bucket_count, head_count = relative_position_bias.shape
    head_size = model_width // head_count
    score_scale = head_size ** (-0.5)
    expert_count = router_weight.shape[1]
    n_expert = lax.axis_size("expert")
    n_fsdp = lax.axis_size("fsdp")
    capacity = 2 * (5 * tok_rows // (4 * n_expert))
    seq_len = tok_rows * n_fsdp
    block_rows = min(512, tok_rows)
    block_count = tok_rows // block_rows
    inputs = tokens.astype(jnp.float32)
    gain_one = norm_gains[0].astype(jnp.float32)
    gain_two = norm_gains[1].astype(jnp.float32)
    normed, inverse_one = norm_forward(inputs, gain_one)
    normed_low = normed.astype(jnp.bfloat16)
    full_qkv, full_out = (
        lax.all_gather(qkv_weight, "fsdp", axis=0, tiled=True),
        lax.all_gather(out_weight, "fsdp", axis=0, tiled=True),
    )
    qkv = jnp.dot(normed_low, full_qkv, preferred_element_type=jnp.float32).astype(jnp.bfloat16)
    key_part = qkv[:, model_width : 2 * model_width]
    value_part = qkv[:, 2 * model_width :]
    all_keys, all_values = (
        lax.all_gather(key_part, "fsdp", axis=0, tiled=True),
        lax.all_gather(value_part, "fsdp", axis=0, tiled=True),
    )
    keys_heads = all_keys.reshape(seq_len, head_count, head_size)
    values_heads = all_values.reshape(seq_len, head_count, head_size)
    queries = qkv[:, :model_width].reshape(block_count, block_rows, head_count, head_size)
    offset = lax.axis_index("fsdp") * tok_rows
    key_pos = jnp.arange(seq_len, dtype=jnp.int32)
    bucket_range = jnp.arange(bucket_count, dtype=jnp.int32)

    def scores_of(block_index, query_block):
        query_pos = offset + block_index * block_rows + jnp.arange(block_rows, dtype=jnp.int32)
        indicator_matrix = (
            bucket_ids(query_pos, key_pos)[None] == bucket_range[:, None, None]
        ).astype(jnp.bfloat16)
        bias_block = jnp.einsum(
            "yur,yv->vur",
            indicator_matrix,
            relative_position_bias,
            preferred_element_type=jnp.float32,
        )
        products = jnp.einsum(
            "qhd,khd->hqk", query_block, keys_heads, preferred_element_type=jnp.float32
        )
        return (products * score_scale + bias_block, indicator_matrix)

    def attend(block_args):
        block_index, query_block = block_args
        scores, indicator_matrix = scores_of(block_index, query_block)
        log_total = jax.nn.logsumexp(scores, axis=-1)
        prob_low = jnp.exp(scores - log_total[..., None]).astype(jnp.bfloat16)
        context = jnp.einsum(
            "hqk,khd->qhd", prob_low, values_heads, preferred_element_type=jnp.float32
        )
        return (context.astype(jnp.bfloat16), log_total)

    block_numbers = jnp.arange(block_count, dtype=jnp.int32)
    context, log_totals = lax.map(attend, (block_numbers, queries))
    context = context.reshape(tok_rows, model_width)
    attention = jnp.dot(context, full_out, preferred_element_type=jnp.float32)
    middle = inputs + attention
    normed_two, inverse_two = norm_forward(middle, gain_two)
    router_float = router_weight.astype(jnp.float32)
    logits = jnp.dot(normed_two, router_float, precision=lax.Precision.HIGHEST)
    router_probs = jax.nn.softmax(logits, axis=-1)
    is_chosen = expert_ids[:, None] == jnp.arange(expert_count, dtype=jnp.int32)[None, :]
    gate_prob = jnp.sum(jnp.where(is_chosen, router_probs, 0.0), axis=1)
    is_kept = slot_ids >= 0
    slot_place = jnp.where(is_kept, expert_ids * capacity + slot_ids, expert_count * capacity)
    safe_place = jnp.where(is_kept, slot_place, 0)
    dispatched = (
        jnp.zeros((expert_count * capacity + 1, model_width), jnp.bfloat16)
        .at[slot_place]
        .set(normed_two.astype(jnp.bfloat16))
    )
    dispatched = dispatched[: expert_count * capacity].reshape(expert_count, capacity, model_width)
    arrived = to_experts(dispatched)
    own_rows = n_expert * capacity
    up_local = up_experts[0]
    down_local = down_experts[0]
    gathered = all_rows(arrived).reshape(-1, model_width)
    pre_act = jnp.dot(gathered, up_local, preferred_element_type=jnp.float32)
    activation_output = gelu_value(pre_act).astype(jnp.bfloat16)

    def down_term(first_row, row_count):
        return jnp.dot(activation_output, down_local, preferred_element_type=jnp.float32)

    partial_out = sum_quarters(down_term, own_rows)
    expert_rows = from_experts(partial_out.reshape(n_expert, capacity, model_width)).reshape(
        -1, model_width
    )
    picked = expert_rows[safe_place]
    expert_mix = jnp.where(is_kept[:, None], gate_prob[:, None] * picked, 0.0)
    block_out = (middle + expert_mix).astype(jnp.bfloat16)
    upstream = cotangent.astype(jnp.float32)
    gate_grad = jnp.where(is_kept, jnp.sum(upstream * picked, axis=1), 0.0)
    grad_rows = jnp.where(is_kept[:, None], gate_prob[:, None] * upstream, 0.0).astype(jnp.bfloat16)
    grad_sent = (
        jnp.zeros((expert_count * capacity + 1, model_width), jnp.bfloat16)
        .at[slot_place]
        .set(grad_rows)
    )
    grad_sent = grad_sent[: expert_count * capacity].reshape(expert_count, capacity, model_width)
    grad_arrived = to_experts(grad_sent)
    grad_gathered = all_rows(grad_arrived).reshape(-1, model_width)
    act_grad = jnp.einsum(
        "rd,hd->rh", grad_gathered, down_local, preferred_element_type=jnp.float32
    )
    pre_grad = (act_grad * gelu_derivative(pre_act)).astype(jnp.bfloat16)
    up_grad = jnp.einsum("rd,rh->dh", gathered, pre_grad, preferred_element_type=jnp.float32)
    down_grad = jnp.einsum(
        "rh,rd->hd", activation_output, grad_gathered, preferred_element_type=jnp.float32
    )

    def up_term(first_row, row_count):
        return jnp.einsum("rh,dh->rd", pre_grad, up_local, preferred_element_type=jnp.float32)

    rows_grad = sum_quarters(up_term, own_rows)
    token_side = from_experts(rows_grad.reshape(n_expert, capacity, model_width)).reshape(
        -1, model_width
    )
    dispatch_grad = jnp.where(is_kept[:, None], token_side[safe_place], 0.0)
    logit_grad = (gate_grad * gate_prob)[:, None] * (is_chosen.astype(jnp.float32) - router_probs)
    router_grad = jnp.dot(normed_two.T, logit_grad, precision=lax.Precision.HIGHEST)
    normed_two_grad = dispatch_grad + jnp.dot(
        logit_grad, router_float.T, precision=lax.Precision.HIGHEST
    )
    middle_part, gain_two_grad = norm_backward(middle, inverse_two, gain_two, normed_two_grad)
    middle_grad = upstream + middle_part
    attention_grad = middle_grad.astype(jnp.bfloat16)
    out_weight_grad = jnp.einsum(
        "td,te->de", context, attention_grad, preferred_element_type=jnp.float32
    )
    context_grad = jnp.einsum(
        "te,de->td", attention_grad, full_out, preferred_element_type=jnp.float32
    ).astype(jnp.bfloat16)
    context_blocks = context_grad.reshape(block_count, block_rows, head_count, head_size)

    def attend_back(carry, block_args):
        key_acc, value_acc, table_acc = carry
        block_index, query_block, grad_block, log_block = block_args
        scores, indicator_matrix = scores_of(block_index, query_block)
        prob_full = jnp.exp(scores - log_block[..., None])
        prob_low = prob_full.astype(jnp.bfloat16)
        prob_grad = jnp.einsum(
            "qhd,khd->hqk", grad_block, values_heads, preferred_element_type=jnp.float32
        )
        attention_score_gradient = (
            prob_full * (prob_grad - jnp.sum(prob_full * prob_grad, axis=-1, keepdims=True))
        ).astype(jnp.bfloat16)
        query_grad = (
            jnp.einsum(
                "hqk,khd->qhd",
                attention_score_gradient,
                keys_heads,
                preferred_element_type=jnp.float32,
            )
            * score_scale
        )
        key_acc = (
            key_acc
            + jnp.einsum(
                "hqk,qhd->khd",
                attention_score_gradient,
                query_block,
                preferred_element_type=jnp.float32,
            )
            * score_scale
        )
        value_acc = value_acc + jnp.einsum(
            "hqk,qhd->khd", prob_low, grad_block, preferred_element_type=jnp.float32
        )
        table_acc = table_acc + jnp.einsum(
            "evf,uvf->eu",
            indicator_matrix,
            attention_score_gradient,
            preferred_element_type=jnp.float32,
        )
        return ((key_acc, value_acc, table_acc), query_grad)

    initial_loop_state = (
        jnp.zeros((seq_len, head_count, head_size), jnp.float32),
        jnp.zeros((seq_len, head_count, head_size), jnp.float32),
        jnp.zeros((bucket_count, head_count), jnp.float32),
    )
    (key_full, value_full, table_grad), query_grads = lax.scan(
        attend_back, initial_loop_state, (block_numbers, queries, context_blocks, log_totals)
    )
    key_own, value_own = (
        lax.psum_scatter(
            key_full.reshape(seq_len, model_width).astype(jnp.bfloat16),
            "fsdp",
            scatter_dimension=0,
            tiled=True,
        ).astype(jnp.float32),
        lax.psum_scatter(
            value_full.reshape(seq_len, model_width).astype(jnp.bfloat16),
            "fsdp",
            scatter_dimension=0,
            tiled=True,
        ).astype(jnp.float32),
    )
    qkv_grad = jnp.concatenate(
        [query_grads.reshape(tok_rows, model_width), key_own, value_own], axis=1
    ).astype(jnp.bfloat16)
    qkv_weight_grad = jnp.einsum(
        "td,te->de", normed_low, qkv_grad, preferred_element_type=jnp.float32
    )
    normed_grad = jnp.einsum("te,de->td", qkv_grad, full_qkv, preferred_element_type=jnp.float32)
    input_part, gain_one_grad = norm_backward(inputs, inverse_one, gain_one, normed_grad)
    tokens_grad = middle_grad + input_part
    total_devices = n_expert * n_fsdp
    own_index = lax.axis_index("expert") * n_fsdp + lax.axis_index("fsdp")
    qkv_sum, out_sum = (
        lax.psum_scatter(
            qkv_weight_grad.reshape(total_devices, -1),
            ("expert", "fsdp"),
            scatter_dimension=0,
            tiled=True,
        ),
        lax.psum_scatter(
            out_weight_grad.reshape(total_devices, -1),
            ("expert", "fsdp"),
            scatter_dimension=0,
            tiled=True,
        ),
    )
    router_sum, gain_sum, table_sum = lax.psum(
        (router_grad, jnp.stack([gain_one_grad, gain_two_grad]), table_grad), ("expert", "fsdp")
    )
    qkv_old = lax.dynamic_slice_in_dim(full_qkv.reshape(total_devices, -1), own_index, 1, 0).astype(
        jnp.float32
    )
    out_old = lax.dynamic_slice_in_dim(full_out.reshape(total_devices, -1), own_index, 1, 0).astype(
        jnp.float32
    )
    qkv_m, qkv_v, qkv_w = adam_step(
        qkv_old, qkv_moment, qkv_square, qkv_sum, 2.0 * model_width ** (-0.5), DECAY
    )
    out_m, out_v, out_w = adam_step(
        out_old, out_moment, out_square, out_sum, (seq_len / model_width) ** 0.5, DECAY
    )
    up_m, up_v, up_w = adam_step(
        up_experts.astype(jnp.float32),
        up_moment,
        up_square,
        up_grad[None],
        2.0 * model_width ** (-0.5),
        DECAY,
    )
    down_m, down_v, down_w = adam_step(
        down_experts.astype(jnp.float32),
        down_moment,
        down_square,
        down_grad[None],
        3.0 * expert_count * FF ** (-0.5),
        DECAY,
    )
    router_m, router_v, router_w = adam_step(
        router_float, router_moment, router_square, router_sum, model_width ** (-0.5), DECAY
    )
    gain_m, gain_v, gain_w = adam_step(
        norm_gains.astype(jnp.float32), gain_moment, gain_square, gain_sum, 0.5, 0.0
    )
    bias_m, bias_v, bias_w = adam_step(
        relative_position_bias.astype(jnp.float32), bias_moment, bias_square, table_sum, 2.0, 0.0
    )
    return (
        block_out,
        tokens_grad,
        qkv_m,
        qkv_v,
        qkv_w,
        out_m,
        out_v,
        out_w,
        up_m,
        up_v,
        up_w,
        down_m,
        down_v,
        down_w,
        router_m,
        router_v,
        router_w,
        gain_m,
        gain_v,
        gain_w,
        bias_m,
        bias_v,
        bias_w,
    )


def solution(mesh):
    return jax.shard_map(
        local,
        mesh=mesh,
        in_specs=(
            P(("expert", "fsdp"), None),
            P(("expert", "fsdp"), None),
            P("fsdp", None),
            P(("expert", "fsdp"), None),
            P(("expert", "fsdp"), None),
            P("fsdp", None),
            P(("expert", "fsdp"), None),
            P(("expert", "fsdp"), None),
            P("expert", None, "fsdp"),
            P("expert", None, "fsdp"),
            P("expert", None, "fsdp"),
            P("expert", "fsdp", None),
            P("expert", "fsdp", None),
            P("expert", "fsdp", None),
            P(),
            P(),
            P(),
            P(),
            P(),
            P(),
            P(),
            P(),
            P(),
            P(("expert", "fsdp")),
            P(("expert", "fsdp")),
        ),
        out_specs=(
            P(("expert", "fsdp"), None),
            P(("expert", "fsdp"), None),
            P(("expert", "fsdp"), None),
            P(("expert", "fsdp"), None),
            P(("expert", "fsdp"), None),
            P(("expert", "fsdp"), None),
            P(("expert", "fsdp"), None),
            P(("expert", "fsdp"), None),
            P("expert", None, "fsdp"),
            P("expert", None, "fsdp"),
            P("expert", None, "fsdp"),
            P("expert", "fsdp", None),
            P("expert", "fsdp", None),
            P("expert", "fsdp", None),
            P(),
            P(),
            P(),
            P(),
            P(),
            P(),
            P(),
            P(),
            P(),
        ),
        check_vma=False,
    )
```

profile of v0, /device:TPU:0, one launch (start us, length us, event | category | flops | bytes accessed | tf_op | source)
XLA Modules:
  0.0 402.4 jit_solution(10607767436580054547)
XLA Ops:
  9.8 1.6 copy.79
  12.0 13.0 %all-gather.3.cloned.1.call-done = bf16[768,2304]{1,0:T(8,128)(2,1)} async-done(((bf16[384,2304]{1,0:T(8,128)(2,1)}), bf16[768,2304]{1,0:T(8,128)(2,1)}) %all-gather.3.cloned.1.call-update) | async-done | bytes 3538960 | tf_op jit(solution)/shard_map/all_gather | solution.py:131
  25.0 2.7 convolution_convert_fusion
  27.8 2.2 all_gather.20
  31.1 2.1 all_gather.19
  34.1 1.6 fusion.110
  37.0 1.7 multiply_reduce_fusion.3
  38.8 1.5 scatter_custom_fusion
  41.3 6.8 %all-to-all-start = ((bf16[16,20,768]{2,1,0:T(8,128)(2,1)}), bf16[16,20,768]{2,1,0:T(8,128)(2,1)S(1)}, u32[]{:S(2)}, u32[]{:S(2)}) async-start(bf16[16,20,768]{2,1,0:T(8,128)(2,1)} %bitcast.7), calls=%async_computation | async-start | bytes 1179648 | tf_op jit(solution)/shard_map/all_to_all | solution.py:63
  48.6 1.4 scatter_custom_fusion.1
  51.8 12.9 %all-to-all-done = bf16[16,20,768]{2,1,0:T(8,128)(2,1)S(1)} async-done(((bf16[16,20,768]{2,1,0:T(8,128)(2,1)}), bf16[16,20,768]{2,1,0:T(8,128)(2,1)S(1)}, u32[]{:S(2)}, u32[]{:S(2)}) %all-to-all-start) | async-done | bytes 491552 | tf_op jit(solution)/shard_map/all_to_all | solution.py:63
  65.5 4.3 %all-to-all-start.2 = ((bf16[16,20,768]{2,1,0:T(8,128)(2,1)}), bf16[16,20,768]{2,1,0:T(8,128)(2,1)}, u32[]{:S(2)}, u32[]{:S(2)}) async-start(bf16[16,20,768]{2,1,0:T(8,128)(2,1)} %bitcast.11), calls=%async_computation.3 | async-start | bytes 1179648 | tf_op jit(solution)/shard_map/all_to_all | solution.py:63
  70.1 2.5 all_gather.22
  73.1 1.1 reshape.229
  74.2 11.3 %all-to-all-done.2 = bf16[16,20,768]{2,1,0:T(8,128)(2,1)} async-done(((bf16[16,20,768]{2,1,0:T(8,128)(2,1)}), bf16[16,20,768]{2,1,0:T(8,128)(2,1)}, u32[]{:S(2)}, u32[]{:S(2)}) %all-to-all-start.2) | async-done | bytes 491552 | tf_op jit(solution)/shard_map/all_to_all | solution.py:63
  85.5 1.1 copy.82
  86.6 2.5 all_gather.23
  89.7 1.2 reshape.235
  90.8 3.7 multiply_convert_fusion
  94.5 1.7 fusion.17
  97.2 1.9 convolution_convert_fusion.1
  99.4 3.1 convolution_convert_fusion.2
  102.5 3.8 reduce-scatter.11.cloned.1.call-done
  106.3 1.9 convert_element_type.217
  108.2 6.8 %all-to-all-start.3 = ((bf16[16,20,768]{2,1,0:T(8,128)(2,1)}), bf16[16,20,768]{2,1,0:T(8,128)(2,1)S(1)}, u32[]{:S(2)}, u32[]{:S(2)}) async-start(bf16[16,20,768]{2,1,0:T(8,128)(2,1)} %convert_element_type.217), calls=%async_computation.5 | async-start | bytes 1179648 | tf_op jit(solution)/shard_map/all_to_all | solution.py:67
  115.0 3.8 reduce-scatter.9.cloned.1.call-done
  118.7 1.9 convert_element_type.211
  120.7 10.9 %all-to-all-done.3 = bf16[16,20,768]{2,1,0:T(8,128)(2,1)S(1)} async-done(((bf16[16,20,768]{2,1,0:T(8,128)(2,1)}), bf16[16,20,768]{2,1,0:T(8,128)(2,1)S(1)}, u32[]{:S(2)}, u32[]{:S(2)}) %all-to-all-start.3) | async-done | bytes 491552 | tf_op jit(solution)/shard_map/all_to_all | solution.py:67
  131.6 4.3 %all-to-all-start.1 = ((bf16[16,20,768]{2,1,0:T(8,128)(2,1)}), bf16[16,20,768]{2,1,0:T(8,128)(2,1)S(1)}, u32[]{:S(2)}, u32[]{:S(2)}) async-start(bf16[16,20,768]{2,1,0:T(8,128)(2,1)} %convert_element_type.211), calls=%async_computation.2 | async-start | bytes 1179648 | tf_op jit(solution)/shard_map/all_to_all | solution.py:67
  136.0 1.3 pad_clamp_fusion
  138.1 1.1 reshape.238
  139.2 12.2 %all-to-all-done.1 = bf16[16,20,768]{2,1,0:T(8,128)(2,1)S(1)} async-done(((bf16[16,20,768]{2,1,0:T(8,128)(2,1)}), bf16[16,20,768]{2,1,0:T(8,128)(2,1)S(1)}, u32[]{:S(2)}, u32[]{:S(2)}) %all-to-all-start.1) | async-done | bytes 491552 | tf_op jit(solution)/shard_map/all_to_all | solution.py:67
  152.3 1.1 reshape.232
  153.5 1.7 gather_fusion.1
  155.2 1.1 gather_fusion
  156.6 2.4 multiply_reduce_fusion.1
  159.0 1.9 convert_add_fusion
  162.9 1.0 fusion.18
  163.9 1.9 copy.86
  165.9 1.2 convolution_convert_fusion.3
  167.1 1.9 copy.88
  169.1 1.9 fusion.76
  171.0 2.9 reshape.242
  174.3 1.1 copy.87
  175.5 8.5 %reduce-scatter.15.cloned.1.call-done = bf16[128,768]{1,0:T(8,128)(2,1)} async-done(((bf16[256,768]{1,0:T(8,128)(2,1)}), bf16[128,768]{1,0:T(8,128)(2,1)}) %reduce-scatter.15.cloned.1.call-update) | async-done | bytes 196624
  184.0 1.1 copy.89
  185.1 4.0 %fusion.47 = f32[768,2304]{1,0:T(8,128)} fusion(bf16[128,768]{0,1:T(8,128)(2,1)S(1)} %copy.89, bf16[128,768]{0,1:T(8,128)(2,1)S(1)} %copy.87, bf16[128,768]{0,1:T(8,128)(2,1)S(1)} %bitcast.100, bf16[128,768]{1,0:T(8,128)(2,1)S(1)} %copy-done.7, f32[768]{0:T(1024)S(1)} %get-tuple-element.100, f32[128]{0:T(128)S(1)} %copy-done.54), kind=kOutput, calls=%fused_computation.93 | convolution fusion | flops 455147520 | bytes 7867904 | tf_op jit(solution)/shard_map/td,te->de/dot_general | solution.py:323
  189.1 6.7 %reshape.240 = f32[32,55296]{1,0:T(8,128)} reshape(f32[768,2304]{1,0:T(8,128)} %fusion.47) | data formatting | bytes 14155776 | tf_op jit(solution)/shard_map/reshape | solution.py:333
  195.9 2.7 reshape.243
  198.5 3.1 reshape.241
  201.7 10.3 %convert_subtract_fusion.1 = (f32[1,768,768]{2,1,0:T(8,128)}, f32[1,768,768]{2,1,0:T(8,128)}, f32[1,768,768]{2,1,0:T(8,128)}) fusion(bf16[1,768,768]{2,1,0:T(8,128)(2,1)} %param.33, f32[1,768,768]{2,1,0:T(8,128)} %param.35, f32[1,768,768]{2,1,0:T(8,128)} %param.34, bf16[640,768]{1,0:T(8,128)(2,1)} %reshape.229, bf16[640,768]{1,0:T(8,128)(2,1)} %copy-done.71), kind=kOutput, calls=%fused_computation.12 | convolution fusion | flops 764411904 | bytes 14942208 | tf_op jit(solution)/shard_map/rd,rh->dh/dot_general | solution.py:227
  212.1 5.7 %convert_subtract_fusion = (f32[1,768,768]{2,1,0:T(8,128)}, f32[1,768,768]{2,1,0:T(8,128)}, f32[1,768,768]{2,1,0:T(8,128)}) fusion(bf16[1,768,768]{2,1,0:T(8,128)(2,1)S(1)} %copy-done.69, f32[1,768,768]{2,1,0:T(8,128)S(1)} %copy-done.64, f32[1,768,768]{2,1,0:T(8,128)S(1)} %copy-done.65, bf16[640,768]{1,0:T(8,128)(2,1)S(1)} %copy-done.70, ...), kind=kOutput, calls=%fused_computation.10 | convolution fusion | flops 764411904 | bytes 14942208 | tf_op jit(solution)/shard_map/rh,rd->hd/dot_general | solution.py:228
  217.7 2.6 copy.85
  220.5 2.9 fusion.26
  223.4 1.0 fusion.41
  224.5 2.6 fusion.36
  227.1 42.7 %all-reduce.2 = (f32[768,8]{0,1:T(8,128)S(1)}, f32[2,768]{1,0:T(2,128)S(1)}, f32[32,12]{0,1:T(8,128)S(1)}) all-reduce(f32[768,8]{0,1:T(8,128)} %fusion.41, f32[2,768]{1,0:T(2,128)S(1)} %pad_maximum_fusion.3, f32[32,12]{0,1:T(8,128)} %fusion.26), channel_id=1, replica_groups=mesh['expert'=16,'fsdp'=2] {'expert','fsdp'}, use_global_device_ids=true, to_apply=%region_21.22 | all-reduce | flops 8064 | bytes 64512 | tf_op jit(solution)/shard_map/psum | solution.py:345
  270.5 1.3 convert_subtract_fusion.4
  271.8 1.3 convert_subtract_fusion.3
  273.2 1.4 convert_subtract_fusion.2
  274.6 2.2 fusion.35
  276.7 112.2 %all-reduce.6.cloned.1.call-done = (f32[32,55296]{1,0:T(8,128)}, f32[32,18432]{1,0:T(8,128)}) async-done(((f32[32,55296]{1,0:T(8,128)}, f32[32,18432]{1,0:T(8,128)}), (f32[32,55296]{1,0:T(8,128)}, f32[32,18432]{1,0:T(8,128)})) %all-reduce.6.cloned.1.call-update) | async-done | bytes 9437200
  388.9 2.4 multiply_subtract_fusion.1
  391.3 4.2 %multiply_subtract_fusion = (f32[1,55296]{1,0:T(1,128)}, f32[1,55296]{1,0:T(1,128)}, f32[1,55296]{1,0:T(1,128)}) fusion(bf16[32,55296]{1,0:T(8,128)(2,1)} %reshape.241, s32[]{:T(128)S(6)} %select_n.70, f32[32,55296]{1,0:T(8,128)} %get-tuple-element.104, u32[]{:T(128)S(6)} %add.350, f32[1,55296]{1,0:T(1,128)S(1)} %copy-done.26, f32[1,55296]{1,0:T(1,128)S(1)} %copy-done.27), kind=kLoop, calls=%fused_computation.96 | loop fusion | flops 884736 | bytes 1437704 | tf_op jit(solution)/shard_map/sub | solution.py:57
  (203 shorter events, 18.2 us)
Async XLA Ops:
  7.2 17.8 %all-gather.3.cloned.1.call-start = ((), (), s32[]{:S(2)}) async-start(), calls=%async_computation.8 | async-start | bytes 5308416 | tf_op jit(solution)/shard_map/all_gather | solution.py:131
  8.0 29.1 %all-gather.5.cloned.1.call-start = ((), (), s32[]{:S(2)}) async-start(), calls=%async_computation.9 | async-start | bytes 1769472 | tf_op jit(solution)/shard_map/all_gather | solution.py:132
  8.9 16.2 %copy-start.53 = (f32[128]{0:T(128)}, f32[128]{0:T(128)S(1)}, u32[]{:S(2)}) copy-start(f32[128]{0:T(128)S(1)} %add_rsqrt_fusion.1) | copy-start | bytes 1540
  27.7 6.4 %copy-start.5 = (f32[128,256,12]{1,0,2:T(8,128)S(1)}, f32[128,256,12]{1,0,2:T(8,128)}, u32[]{:S(2)}) copy-start(f32[128,256,12]{1,0,2:T(8,128)} %copy.79) | copy-start | bytes 4718596
  36.7 4.6 %copy-start.13 = (bf16[12,64,128]{2,1,0:T(8,128)(2,1)}, bf16[12,64,128]{2,1,0:T(8,128)(2,1)S(1)}, u32[]{:S(2)}) copy-start(bf16[12,64,128]{2,1,0:T(8,128)(2,1)S(1)} %convolution_convert_fusion.5) | copy-start | bytes 589828
  38.7 120.2 %copy-start.1 = (f32[128,768]{1,0:T(8,128)}, f32[128,768]{1,0:T(8,128)S(1)}, u32[]{:S(2)}) copy-start(f32[128,768]{1,0:T(8,128)S(1)} %get-tuple-element.137) | copy-start | bytes 1179652
  38.7 9.3 %copy-start.62 = (s32[128]{0:T(128)S(1)}, s32[128]{0:T(128)}, u32[]{:S(2)}) copy-start(s32[128]{0:T(128)} %param.49) | copy-start | bytes 1540
  38.8 9.3 %copy-start.28 = (bf16[768,8]{0,1:T(8,128)(2,1)S(1)}, bf16[768,8]{0,1:T(8,128)(2,1)}, u32[]{:S(2)}) copy-start(bf16[768,8]{0,1:T(8,128)(2,1)} %param.39) | copy-start | bytes 36868
  38.8 9.7 %copy-start.38 = (f32[128]{0:T(128)}, f32[128]{0:T(128)S(1)}, u32[]{:S(2)}) copy-start(f32[128]{0:T(128)S(1)} %add_rsqrt_fusion) | copy-start | bytes 1540
  38.8 9.8 %copy-start.48 = (s32[128]{0:T(128)S(1)}, s32[128]{0:T(128)}, u32[]{:S(2)}) copy-start(s32[128]{0:T(128)} %param.48) | copy-start | bytes 1540
  38.8 9.8 %copy-start.15 = (bf16[128,768]{1,0:T(8,128)(2,1)S(1)}, bf16[128,768]{1,0:T(8,128)(2,1)}, u32[]{:S(2)}) copy-start(bf16[128,768]{1,0:T(8,128)(2,1)} %param.26) | copy-start | bytes 589828
  41.3 23.4 %all-to-all-start = ((bf16[16,20,768]{2,1,0:T(8,128)(2,1)}), bf16[16,20,768]{2,1,0:T(8,128)(2,1)S(1)}, u32[]{:S(2)}, u32[]{:S(2)}) async-start(bf16[16,20,768]{2,1,0:T(8,128)(2,1)} %bitcast.7), calls=%async_computation | async-start | bytes 1179648 | tf_op jit(solution)/shard_map/all_to_all | solution.py:63
  48.1 17.4 %copy-start.57 = (pred[128]{0:T(512)(128)(4,1)}, pred[128]{0:T(512)(128)(4,1)S(1)}, u32[]{:S(2)}) copy-start(pred[128]{0:T(512)(128)(4,1)S(1)} %broadcast_compare_fusion) | copy-start | bytes 388
  48.5 21.4 %copy-start.30 = (f32[128,8]{0,1:T(8,128)}, f32[128,8]{0,1:T(8,128)S(1)}, u32[]{:S(2)}) copy-start(f32[128,8]{0,1:T(8,128)S(1)} %get-tuple-element.139) | copy-start | bytes 12292
  48.5 21.3 %copy-start.41 = (f32[128]{0:T(128)}, f32[128]{0:T(128)S(1)}, u32[]{:S(2)}) copy-start(f32[128]{0:T(128)S(1)} %get-tuple-element.138) | copy-start | bytes 1540
  48.6 21.3 %copy-start.44 = (f32[128]{0:T(128)}, f32[128]{0:T(128)S(1)}, u32[]{:S(2)}) copy-start(f32[128]{0:T(128)S(1)} %fusion.93) | copy-start | bytes 1540
  48.6 21.3 %copy-start.51 = (f32[128]{0:T(128)}, f32[128]{0:T(128)S(1)}, u32[]{:S(2)}) copy-start(f32[128]{0:T(128)S(1)} %select_reduce_fusion) | copy-start | bytes 1540
  65.5 19.9 %all-to-all-start.2 = ((bf16[16,20,768]{2,1,0:T(8,128)(2,1)}), bf16[16,20,768]{2,1,0:T(8,128)(2,1)}, u32[]{:S(2)}, u32[]{:S(2)}) async-start(bf16[16,20,768]{2,1,0:T(8,128)(2,1)} %bitcast.11), calls=%async_computation.3 | async-start | bytes 1179648 | tf_op jit(solution)/shard_map/all_to_all | solution.py:63
  69.9 36.3 %reduce-scatter.11.cloned.1.call-start = ((), (), s32[]{:S(2)}) async-start(), calls=%async_computation.11 | async-start | bytes 1474560 | tf_op jit(solution)/shard_map/reduce_scatter | solution.py:79
  90.8 3.7 copy-start.17
  90.8 3.7 copy-start.67
  94.5 2.7 copy-start.66
  99.1 19.6 %reduce-scatter.9.cloned.1.call-start = ((), (), s32[]{:S(2)}) async-start(), calls=%async_computation.10 | async-start | bytes 1474560 | tf_op jit(solution)/shard_map/reduce_scatter | solution.py:79
  108.2 23.4 %all-to-all-start.3 = ((bf16[16,20,768]{2,1,0:T(8,128)(2,1)}), bf16[16,20,768]{2,1,0:T(8,128)(2,1)S(1)}, u32[]{:S(2)}, u32[]{:S(2)}) async-start(bf16[16,20,768]{2,1,0:T(8,128)(2,1)} %convert_element_type.217), calls=%async_computation.5 | async-start | bytes 1179648 | tf_op jit(solution)/shard_map/all_to_all | solution.py:67
  131.6 19.8 %all-to-all-start.1 = ((bf16[16,20,768]{2,1,0:T(8,128)(2,1)}), bf16[16,20,768]{2,1,0:T(8,128)(2,1)S(1)}, u32[]{:S(2)}, u32[]{:S(2)}) async-start(bf16[16,20,768]{2,1,0:T(8,128)(2,1)} %convert_element_type.211), calls=%async_computation.2 | async-start | bytes 1179648 | tf_op jit(solution)/shard_map/all_to_all | solution.py:67
  135.9 38.4 %reduce-scatter.13.cloned.1.call-start = ((), (), s32[]{:S(2)}) async-start(), calls=%async_computation.12 | async-start | bytes 589824
  156.3 2.6 copy-start.12
  156.3 4.6 %copy-start.4 = (bf16[768,768]{1,0:T(8,128)(2,1)S(1)}, bf16[768,768]{1,0:T(8,128)(2,1)}, u32[]{:S(2)}) copy-start(bf16[768,768]{1,0:T(8,128)(2,1)} %all-gather.5.cloned.1.call-done) | copy-start | bytes 3538948
  156.6 2.4 copy-start.59
  159.0 2.7 copy-start.11
  160.9 8.2 %copy-start.6 = (f32[128,768]{1,0:T(8,128)}, f32[128,768]{1,0:T(8,128)S(1)}, u32[]{:S(2)}) copy-start(f32[128,768]{1,0:T(8,128)S(1)} %get-tuple-element.130) | copy-start | bytes 1179652
  162.9 11.0 %copy-start.3 = (bf16[12,128,256]{2,1,0:T(8,128)(2,1)}, bf16[12,128,256]{2,1,0:T(8,128)(2,1)S(1)}, u32[]{:S(2)}) copy-start(bf16[12,128,256]{2,1,0:T(8,128)(2,1)S(1)} %multiply_convert_fusion.1) | copy-start | bytes 2359300
  165.8 3.3 copy-start.14
  165.8 18.2 %reduce-scatter.15.cloned.1.call-start = ((), (), s32[]{:S(2)}) async-start(), calls=%async_computation.13 | async-start | bytes 589824
  169.0 219.9 %all-reduce.6.cloned.1.call-start = ((), (), s32[]{:S(2)}) async-start(), calls=%async_computation.14 | async-start | bytes 18874368
  171.0 2.9 copy-start.9
  173.9 11.2 %copy-start.54 = (f32[128]{0:T(128)S(1)}, f32[128]{0:T(128)}, u32[]{:S(2)}) copy-start(f32[128]{0:T(128)} %copy-done.53) | copy-start | bytes 1540
  174.3 14.8 %copy-start.23 = (bf16[12,64,128]{2,1,0:T(8,128)(2,1)}, bf16[12,64,128]{2,1,0:T(8,128)(2,1)S(1)}, u32[]{:S(2)}) copy-start(bf16[12,64,128]{2,1,0:T(8,128)(2,1)S(1)} %fusion.25) | copy-start | bytes 589828
  175.5 13.7 %copy-start.19 = (bf16[128,768]{0,1:T(8,128)(2,1)}, bf16[128,768]{0,1:T(8,128)(2,1)S(1)}, u32[]{:S(2)}) copy-start(bf16[128,768]{0,1:T(8,128)(2,1)S(1)} %copy.87) | copy-start | bytes 589828
  185.1 4.1 %copy-start.21 = (bf16[128,768]{0,1:T(8,128)(2,1)}, bf16[128,768]{0,1:T(8,128)(2,1)S(1)}, u32[]{:S(2)}) copy-start(bf16[128,768]{0,1:T(8,128)(2,1)S(1)} %copy.89) | copy-start | bytes 589828
  195.8 2.7 copy-start
  201.6 10.4 %copy-start.18 = (bf16[640,768]{1,0:T(8,128)(2,1)S(1)}, bf16[640,768]{1,0:T(8,128)(2,1)}, u32[]{:S(2)}) copy-start(bf16[640,768]{1,0:T(8,128)(2,1)} %reshape.235) | copy-start | bytes 2949124
  201.6 10.4 %copy-start.64 = (f32[1,768,768]{2,1,0:T(8,128)S(1)}, f32[1,768,768]{2,1,0:T(8,128)}, u32[]{:S(2)}) copy-start(f32[1,768,768]{2,1,0:T(8,128)} %param.38) | copy-start | bytes 7077892
  201.6 10.4 %copy-start.65 = (f32[1,768,768]{2,1,0:T(8,128)S(1)}, f32[1,768,768]{2,1,0:T(8,128)}, u32[]{:S(2)}) copy-start(f32[1,768,768]{2,1,0:T(8,128)} %param.37) | copy-start | bytes 7077892
  201.7 10.4 %copy-start.69 = (bf16[1,768,768]{2,1,0:T(8,128)(2,1)S(1)}, bf16[1,768,768]{2,1,0:T(8,128)(2,1)}, u32[]{:S(2)}) copy-start(bf16[1,768,768]{2,1,0:T(8,128)(2,1)} %param.36) | copy-start | bytes 3538948
  201.7 10.4 %copy-start.70 = (bf16[640,768]{1,0:T(8,128)(2,1)S(1)}, bf16[640,768]{1,0:T(8,128)(2,1)}, u32[]{:S(2)}) copy-start(bf16[640,768]{1,0:T(8,128)(2,1)} %get-tuple-element.140) | copy-start | bytes 2949124
  212.0 8.4 %copy-start.35 = (f32[768]{0:T(1024)S(1)}, f32[768]{0:T(1024)}, u32[]{:S(2)}) copy-start(f32[768]{0:T(1024)} %get-tuple-element.81) | copy-start | bytes 9220
  217.7 5.6 %copy-start.32 = (f32[128,8]{0,1:T(8,128)S(1)}, f32[128,8]{0,1:T(8,128)}, u32[]{:S(2)}) copy-start(f32[128,8]{0,1:T(8,128)} %copy-done.30) | copy-start | bytes 12292
  220.4 3.0 copy-start.2
  220.4 3.0 copy-start.40
  220.4 3.0 copy-start.43
  220.4 3.0 copy-start.46
  220.4 3.0 copy-start.50
  220.4 3.0 copy-start.60
  220.4 4.1 %copy-start.8 = (bf16[128,768]{1,0:T(8,128)(2,1)S(1)}, bf16[128,768]{1,0:T(8,128)(2,1)}, u32[]{:S(2)}) copy-start(bf16[128,768]{1,0:T(8,128)(2,1)} %param.25) | copy-start | bytes 589828
  220.4 4.1 %copy-start.20 = (bf16[128,768]{0,1:T(8,128)(2,1)S(1)}, bf16[128,768]{0,1:T(8,128)(2,1)}, u32[]{:S(2)}) copy-start(bf16[128,768]{0,1:T(8,128)(2,1)} %copy-done.19) | copy-start | bytes 589828
  220.4 4.1 %copy-start.22 = (bf16[128,768]{0,1:T(8,128)(2,1)S(1)}, bf16[128,768]{0,1:T(8,128)(2,1)}, u32[]{:S(2)}) copy-start(bf16[128,768]{0,1:T(8,128)(2,1)} %copy-done.21) | copy-start | bytes 589828
  220.4 4.0 %copy-start.24 = (bf16[12,64,128]{2,1,0:T(8,128)(2,1)S(1)}, bf16[12,64,128]{2,1,0:T(8,128)(2,1)}, u32[]{:S(2)}) copy-start(bf16[12,64,128]{2,1,0:T(8,128)(2,1)} %copy-done.23) | copy-start | bytes 589828
  220.4 4.0 %copy-start.55 = (f32[128]{0:T(128)S(1)}, f32[128]{0:T(128)}, u32[]{:S(2)}) copy-start(f32[128]{0:T(128)} %copy-done.53) | copy-start | bytes 1540
  224.5 46.0 %copy-start.34 = (bf16[2,768]{1,0:T(2,128)(2,1)S(1)}, bf16[2,768]{1,0:T(2,128)(2,1)}, u32[]{:S(2)}) copy-start(bf16[2,768]{1,0:T(2,128)(2,1)} %param.42) | copy-start | bytes 9220
  224.5 47.3 %copy-start.37 = (bf16[32,12]{0,1:T(8,128)(2,1)S(1)}, bf16[32,12]{0,1:T(8,128)(2,1)}, u32[]{:S(2)}) copy-start(bf16[32,12]{0,1:T(8,128)(2,1)} %param.45) | copy-start | bytes 2308
  224.5 50.1 %copy-start.56 = (f32[128]{0:T(128)S(1)}, f32[128]{0:T(128)}, u32[]{:S(2)}) copy-start(f32[128]{0:T(128)} %copy-done.53) | copy-start | bytes 1540
  227.1 164.2 %copy-start.26 = (f32[1,55296]{1,0:T(1,128)S(1)}, f32[1,55296]{1,0:T(1,128)}, u32[]{:S(2)}) copy-start(f32[1,55296]{1,0:T(1,128)} %param.29) | copy-start | bytes 663556
  227.1 164.2 %copy-start.27 = (f32[1,55296]{1,0:T(1,128)S(1)}, f32[1,55296]{1,0:T(1,128)}, u32[]{:S(2)}) copy-start(f32[1,55296]{1,0:T(1,128)} %param.28) | copy-start | bytes 663556
  (19 other events, 29.0 us)
Sparse Core Ops, SparseCore 0:
  9.6 15.3 all-gather.2
  26.6 10.3 all-gather.4
  99.3 6.9 reduce-scatter.10
  109.1 9.6 reduce-scatter.8
  165.9 6.2 reduce-scatter.12
  175.0 8.9 reduce-scatter.14
  196.0 192.9 all-reduce.5
where the time goes:
time: 404 us; the launch traced here: 402 us
  waiting for transfers between devices  190 us (47%)
  matrix products  52.6 us (13%)
  blocking collectives  52 us (13%)
  local copies, waits for them, and re-layouts  46.2 us (11%)
  other arithmetic  23.5 us (6%)
  starting transfers between devices  22.7 us (6%)
  between operations  15.2 us (4%)
    unnamed x10, waiting for transfers between devices  122 us
    psum x1, blocking collectives, local(): lax.psum((router_grad, jnp.stack([gain_one_grad, gain_two_grad]), table_g...  42.7 us
    all_to_all x2, waiting for transfers between devices, to_experts(): lax.all_to_all(doubled, 'expert', split_axis=0, concat_axis=0, tiled=True)  24.2 us
    all_to_all x2, waiting for transfers between devices, from_experts(): lax.all_to_all(partial_rows.astype(jnp.bfloat16), 'expert', split_axis=0,...  23.1 us
    all_gather x1, waiting for transfers between devices, local(): lax.all_gather(qkv_weight, 'fsdp', axis=0, tiled=True)  13 us
    all_to_all x2, starting transfers between devices, to_experts(): lax.all_to_all(doubled, 'expert', split_axis=0, concat_axis=0, tiled=True)  11.1 us
    all_to_all x2, starting transfers between devices, from_experts(): lax.all_to_all(partial_rows.astype(jnp.bfloat16), 'expert', split_axis=0,...  11.1 us
    sub x5, other arithmetic, adam_step(): weight - rate * (moment_hat / (jnp.sqrt(square_hat) + ADAM_EPS) + decay *...  10.7 us
  transfers between devices with their start and end apart: 11, of which 10 were waited for; matrix products, arithmetic and copies ran while one was open for 18% of the time, Pallas kernels for 0%

commit v1 on v0

v1 whole, which is shorter than its diff:
```python
import jax
import jax.numpy as jnp
from jax import lax
from jax.sharding import PartitionSpec as P

FF = 3072
STEP = 10


EPS_NORM = 1e-06
BETA_ONE = 0.9
BETA_TWO = 0.999
ADAM_EPS = 1e-08
DECAY = 0.1
ROOT_HALF = 0.7071067811865476
INV_ROOT_TWO_PI = 0.3989422804014327


def norm_forward(value, gain):
    inverse = lax.rsqrt(jnp.mean(value * value, axis=-1, keepdims=True) + EPS_NORM)
    return (value * inverse * gain, inverse)


def norm_backward(value, inverse, gain, upstream):
    scaled = upstream * gain
    normal = value * inverse
    gain_grad = jnp.sum(normal * upstream, axis=0)
    value_grad = inverse * (scaled - normal * jnp.mean(normal * scaled, axis=-1, keepdims=True))
    return (value_grad, gain_grad)


def gelu_value(value):
    return 0.5 * value * (1.0 + lax.erf(value * ROOT_HALF))


def gelu_derivative(value):
    return (
        0.5 * (1.0 + lax.erf(value * ROOT_HALF))
        + value * jnp.exp(-0.5 * value * value) * INV_ROOT_TWO_PI
    )


def bucket_ids(query_pos, key_pos):
    relative = key_pos[None, :] - query_pos[:, None]
    distance = jnp.abs(relative)
    far_bucket = jnp.full(distance.shape, 8, jnp.int32)
    for degree in range(1, 8):
        far_bucket = far_bucket + (distance * distance >= 2 ** (degree + 6)).astype(jnp.int32)
    return jnp.where(distance < 8, distance, far_bucket) + 16 * (relative > 0).astype(jnp.int32)


def adam_step(weight, moment, square, grad, rate, decay):
    new_moment = BETA_ONE * moment + (1.0 - BETA_ONE) * grad
    new_square = BETA_TWO * square + (1.0 - BETA_TWO) * grad * grad
    moment_hat = new_moment / (1.0 - BETA_ONE**STEP)
    square_hat = new_square / (1.0 - BETA_TWO**STEP)
    new_weight = weight - rate * (moment_hat / (jnp.sqrt(square_hat) + ADAM_EPS) + decay * weight)
    return (new_moment, new_square, new_weight)


def swap(value):
    return lax.ppermute(value, "fsdp", ((0, 1), (1, 0)))


def bit_swap(value, bit):
    size = lax.axis_size("expert")
    return lax.ppermute(value, "expert", tuple((i, i ^ (1 << bit)) for i in range(size)))


def sum_to_owner(grad, order):
    n_expert = lax.axis_size("expert")
    bits = n_expert.bit_length() - 1
    rows, columns = grad.shape
    block = rows // (2 * n_expert)
    core = lax.axis_index("fsdp")
    place = lax.axis_index("expert")
    pieces = grad.reshape((n_expert, 2, block, columns))
    kept = lax.dynamic_index_in_dim(pieces, core, 1, keepdims=False)
    sent = lax.dynamic_index_in_dim(pieces, 1 - core, 1, keepdims=False)
    total = kept + swap(sent.astype(jnp.bfloat16)).astype(jnp.float32)
    total = total.reshape((2,) * bits + (block, columns))
    left = list(range(bits - 1, -1, -1))
    for bit in order:
        axis = left.index(bit)
        left.remove(bit)
        mine = (place >> bit) & 1
        sent = lax.dynamic_index_in_dim(total, 1 - mine, axis, keepdims=False)
        kept = lax.dynamic_index_in_dim(total, mine, axis, keepdims=False)
        total = kept + bit_swap(sent.astype(jnp.bfloat16), bit).astype(jnp.float32)
    return total


def sum_everywhere(value):
    bits = lax.axis_size("expert").bit_length() - 1
    value = value + swap(value)
    for bit in range(bits):
        value = value + bit_swap(value, bit)
    return value


def local(
    tokens,
    cotangent,
    qkv_weight,
    qkv_moment,
    qkv_square,
    out_weight,
    out_moment,
    out_square,
    up_experts,
    up_moment,
    up_square,
    down_experts,
    down_moment,
    down_square,
    router_weight,
    router_moment,
    router_square,
    norm_gains,
    gain_moment,
    gain_square,
    relative_position_bias,
    bias_moment,
    bias_square,
    expert_ids,
    slot_ids,
):
    tok_rows, model_width = tokens.shape
    bucket_count, head_count = relative_position_bias.shape
    head_size = model_width // head_count
    score_scale = head_size ** (-0.5)
    expert_count = router_weight.shape[1]
    n_expert = lax.axis_size("expert")
    n_fsdp = lax.axis_size("fsdp")
    bits = n_expert.bit_length() - 1
    capacity = 2 * (5 * tok_rows // (4 * n_expert))
    seq_len = tok_rows * n_fsdp
    half = model_width // 2
    core = lax.axis_index("fsdp")
    own_index = lax.axis_index("expert") * n_fsdp + core
    qkv_other = swap(qkv_weight)
    out_other = swap(out_weight)
    inputs = tokens.astype(jnp.float32)
    upstream = cotangent.astype(jnp.float32)
    gain_one = norm_gains[0].astype(jnp.float32)
    gain_two = norm_gains[1].astype(jnp.float32)
    normed, inverse_one = norm_forward(inputs, gain_one)
    normed_low = normed.astype(jnp.bfloat16)

    def own_part(value):
        return lax.dynamic_slice_in_dim(value, core * half, half, 1)

    def other_part(value):
        return lax.dynamic_slice_in_dim(value, (1 - core) * half, half, 1)

    def times_halves(value, own, other):
        return jnp.dot(own_part(value), own, preferred_element_type=jnp.float32) + jnp.dot(
            other_part(value), other, preferred_element_type=jnp.float32
        )

    def times_transposed(value, own, other):
        first = jnp.where(core == 0, own, other)
        second = jnp.where(core == 0, other, own)
        return jnp.concatenate(
            [
                jnp.einsum("te,de->td", value, first, preferred_element_type=jnp.float32),
                jnp.einsum("te,de->td", value, second, preferred_element_type=jnp.float32),
            ],
            axis=1,
        )

    query_pos = core * tok_rows + jnp.arange(tok_rows, dtype=jnp.int32)
    other_pos = (1 - core) * tok_rows + jnp.arange(tok_rows, dtype=jnp.int32)
    key_pos = jnp.concatenate([query_pos, other_pos])
    bucket_range = jnp.arange(bucket_count, dtype=jnp.int32)
    indicator = (bucket_ids(query_pos, key_pos)[None] == bucket_range[:, None, None]).astype(
        jnp.bfloat16
    )
    bias_block = jnp.einsum(
        "yur,yv->vur", indicator, relative_position_bias, preferred_element_type=jnp.float32
    )
    qkv = times_halves(normed_low, qkv_weight, qkv_other).astype(jnp.bfloat16)
    key_value = qkv[:, model_width:]
    both = jnp.concatenate([key_value, swap(key_value)], axis=0)
    keys_heads = both[:, :model_width].reshape(seq_len, head_count, head_size)
    values_heads = both[:, model_width:].reshape(seq_len, head_count, head_size)
    queries = qkv[:, :model_width].reshape(tok_rows, head_count, head_size)
    scores = (
        jnp.einsum("qhd,khd->hqk", queries, keys_heads, preferred_element_type=jnp.float32)
        * score_scale
        + bias_block
    )
    log_total = jax.nn.logsumexp(scores, axis=-1, keepdims=True)
    prob_full = jnp.exp(scores - log_total)
    prob_low = prob_full.astype(jnp.bfloat16)
    context = (
        jnp.einsum("hqk,khd->qhd", prob_low, values_heads, preferred_element_type=jnp.float32)
        .astype(jnp.bfloat16)
        .reshape(tok_rows, model_width)
    )
    attention = times_halves(context, out_weight, out_other)
    middle = inputs + attention
    normed_two, inverse_two = norm_forward(middle, gain_two)
    router_float = router_weight.astype(jnp.float32)
    logits = jnp.dot(normed_two, router_float, precision=lax.Precision.HIGHEST)
    router_probs = jax.nn.softmax(logits, axis=-1)
    is_chosen = expert_ids[:, None] == jnp.arange(expert_count, dtype=jnp.int32)[None, :]
    gate_prob = jnp.sum(jnp.where(is_chosen, router_probs, 0.0), axis=1)
    slot_rows = n_expert * capacity
    row_range = jnp.arange(slot_rows, dtype=jnp.int32)
    row_expert = row_range // (2 * capacity)
    row_slot = row_range % capacity
    pick = (
        (row_expert[None, :] == expert_ids[:, None]) & (row_slot[None, :] == slot_ids[:, None])
    ).astype(jnp.bfloat16)
    token_rows = jnp.concatenate(
        [normed_two.astype(jnp.bfloat16), (gate_prob[:, None] * upstream).astype(jnp.bfloat16)],
        axis=1,
    )
    dispatched = jnp.einsum(
        "tr,td->rd", pick, token_rows, preferred_element_type=jnp.float32
    ).astype(jnp.bfloat16)
    arrived = lax.all_to_all(
        dispatched.reshape(n_expert, capacity, 2 * model_width),
        "expert",
        split_axis=0,
        concat_axis=0,
        tiled=True,
    ).reshape(slot_rows, 2 * model_width)
    up_local = up_experts[0]
    down_local = down_experts[0]
    gathered = jnp.concatenate([arrived, swap(arrived)], axis=0)
    expert_in = gathered[:, :model_width]
    grad_in = gathered[:, model_width:]
    pre_act = jnp.dot(expert_in, up_local, preferred_element_type=jnp.float32)
    activated = gelu_value(pre_act).astype(jnp.bfloat16)
    act_grad = jnp.einsum("rd,hd->rh", grad_in, down_local, preferred_element_type=jnp.float32)
    pre_grad = (act_grad * gelu_derivative(pre_act)).astype(jnp.bfloat16)
    partial_rows = jnp.concatenate(
        [
            jnp.dot(activated, down_local, preferred_element_type=jnp.float32),
            jnp.einsum("rh,dh->rd", pre_grad, up_local, preferred_element_type=jnp.float32),
        ],
        axis=1,
    )
    from_other = swap(partial_rows[slot_rows:].astype(jnp.bfloat16))
    summed = (partial_rows[:slot_rows] + from_other.astype(jnp.float32)).astype(jnp.bfloat16)
    returned = lax.all_to_all(
        summed.reshape(n_expert, capacity, 2 * model_width),
        "expert",
        split_axis=0,
        concat_axis=0,
        tiled=True,
    ).reshape(slot_rows, 2 * model_width)
    up_grad = jnp.einsum("rd,rh->dh", expert_in, pre_grad, preferred_element_type=jnp.float32)
    down_grad = jnp.einsum("rh,rd->hd", activated, grad_in, preferred_element_type=jnp.float32)
    mixed = jnp.dot(pick, returned, preferred_element_type=jnp.float32)
    picked = mixed[:, :model_width]
    dispatch_grad = mixed[:, model_width:]
    block_out = (middle + gate_prob[:, None] * picked).astype(jnp.bfloat16)
    gate_grad = jnp.sum(upstream * picked, axis=1)
    logit_grad = (gate_grad * gate_prob)[:, None] * (is_chosen.astype(jnp.float32) - router_probs)
    router_grad = jnp.dot(logit_grad.T, normed_two, precision=lax.Precision.HIGHEST)
    normed_two_grad = dispatch_grad + jnp.dot(
        logit_grad, router_float.T, precision=lax.Precision.HIGHEST
    )
    middle_part, gain_two_grad = norm_backward(middle, inverse_two, gain_two, normed_two_grad)
    middle_grad = upstream + middle_part
    attention_grad = middle_grad.astype(jnp.bfloat16)
    out_weight_grad = jnp.einsum(
        "td,te->de", context, attention_grad, preferred_element_type=jnp.float32
    )
    context_grad = (
        times_transposed(attention_grad, out_weight, out_other)
        .astype(jnp.bfloat16)
        .reshape(tok_rows, head_count, head_size)
    )
    prob_grad = jnp.einsum(
        "qhd,khd->hqk", context_grad, values_heads, preferred_element_type=jnp.float32
    )
    score_grad = (
        prob_full * (prob_grad - jnp.sum(prob_full * prob_grad, axis=-1, keepdims=True))
    ).astype(jnp.bfloat16)
    value_grad = jnp.einsum(
        "hqk,qhd->khd", prob_low, context_grad, preferred_element_type=jnp.float32
    ).reshape(seq_len, model_width)
    key_grad = (
        jnp.einsum("hqk,qhd->khd", score_grad, queries, preferred_element_type=jnp.float32)
        * score_scale
    ).reshape(seq_len, model_width)
    key_value_grad = jnp.concatenate([key_grad, value_grad], axis=1)
    key_value_own = (
        key_value_grad[:tok_rows]
        + swap(key_value_grad[tok_rows:].astype(jnp.bfloat16)).astype(jnp.float32)
    ).astype(jnp.bfloat16)
    query_grad = (
        (
            jnp.einsum("hqk,khd->qhd", score_grad, keys_heads, preferred_element_type=jnp.float32)
            * score_scale
        )
        .astype(jnp.bfloat16)
        .reshape(tok_rows, model_width)
    )
    table_grad = jnp.einsum(
        "evf,uvf->eu", indicator, score_grad, preferred_element_type=jnp.float32
    )
    qkv_grad = jnp.concatenate([query_grad, key_value_own], axis=1)

    def weight_grad(upstream_part):
        return jnp.einsum(
            "td,te->de", normed_low, upstream_part, preferred_element_type=jnp.float32
        )

    upward = list(range(bits))
    out_sum = sum_to_owner(out_weight_grad, upward[2:] + upward[:2])
    query_sum = sum_to_owner(weight_grad(query_grad), upward)
    key_sum = sum_to_owner(
        weight_grad(key_value_own[:, :model_width]), upward[1:] + upward[:1]
    )
    value_sum = sum_to_owner(
        weight_grad(key_value_own[:, model_width:]), upward[2:] + upward[:2]
    )
    normed_grad = times_transposed(qkv_grad, qkv_weight, qkv_other)
    input_part, gain_one_grad = norm_backward(inputs, inverse_one, gain_one, normed_grad)
    tokens_grad = middle_grad + input_part
    table_size = bucket_count * head_count
    small = jnp.concatenate(
        [
            router_grad,
            gain_one_grad[None],
            gain_two_grad[None],
            jnp.pad(table_grad.reshape(1, table_size), ((0, 0), (0, model_width - table_size))),
        ],
        axis=0,
    )
    small = sum_everywhere(small)
    router_sum = small[:expert_count].T
    gain_sum = small[expert_count : expert_count + 2]
    table_sum = small[expert_count + 2, :table_size].reshape(bucket_count, head_count)
    qkv_sum = jnp.concatenate([query_sum, key_sum, value_sum], axis=1).reshape(1, -1)
    block = model_width // (n_expert * n_fsdp)
    first_row = own_index * block
    owner_core = first_row // half
    local_row = first_row - owner_core * half

    def old_rows(own, other):
        own_rows = lax.dynamic_slice_in_dim(own, local_row, block, 0)
        other_rows = lax.dynamic_slice_in_dim(other, local_row, block, 0)
        rows = jnp.where(owner_core == core, own_rows, other_rows)
        return rows.astype(jnp.float32).reshape(1, -1)

    qkv_old = old_rows(qkv_weight, qkv_other)
    out_old = old_rows(out_weight, out_other)
    out_sum = out_sum.reshape(1, -1)
    qkv_m, qkv_v, qkv_w = adam_step(
        qkv_old, qkv_moment, qkv_square, qkv_sum, 2.0 * model_width ** (-0.5), DECAY
    )
    out_m, out_v, out_w = adam_step(
        out_old, out_moment, out_square, out_sum, (seq_len / model_width) ** 0.5, DECAY
    )
    up_m, up_v, up_w = adam_step(
        up_experts.astype(jnp.float32),
        up_moment,
        up_square,
        up_grad[None],
        2.0 * model_width ** (-0.5),
        DECAY,
    )
    down_m, down_v, down_w = adam_step(
        down_experts.astype(jnp.float32),
        down_moment,
        down_square,
        down_grad[None],
        3.0 * expert_count * FF ** (-0.5),
        DECAY,
    )
    router_m, router_v, router_w = adam_step(
        router_float, router_moment, router_square, router_sum, model_width ** (-0.5), DECAY
    )
    gain_m, gain_v, gain_w = adam_step(
        norm_gains.astype(jnp.float32), gain_moment, gain_square, gain_sum, 0.5, 0.0
    )
    bias_m, bias_v, bias_w = adam_step(
        relative_position_bias.astype(jnp.float32), bias_moment, bias_square, table_sum, 2.0, 0.0
    )
    return (
        block_out,
        tokens_grad,
        qkv_m,
        qkv_v,
        qkv_w,
        out_m,
        out_v,
        out_w,
        up_m,
        up_v,
        up_w,
        down_m,
        down_v,
        down_w,
        router_m,
        router_v,
        router_w,
        gain_m,
        gain_v,
        gain_w,
        bias_m,
        bias_v,
        bias_w,
    )


def solution(mesh):
    return jax.shard_map(
        local,
        mesh=mesh,
        in_specs=(
            P(("expert", "fsdp"), None),
            P(("expert", "fsdp"), None),
            P("fsdp", None),
            P(("expert", "fsdp"), None),
            P(("expert", "fsdp"), None),
            P("fsdp", None),
            P(("expert", "fsdp"), None),
            P(("expert", "fsdp"), None),
            P("expert", None, "fsdp"),
            P("expert", None, "fsdp"),
            P("expert", None, "fsdp"),
            P("expert", "fsdp", None),
            P("expert", "fsdp", None),
            P("expert", "fsdp", None),
            P(),
            P(),
            P(),
            P(),
            P(),
            P(),
            P(),
            P(),
            P(),
            P(("expert", "fsdp")),
            P(("expert", "fsdp")),
        ),
        out_specs=(
            P(("expert", "fsdp"), None),
            P(("expert", "fsdp"), None),
            P(("expert", "fsdp"), None),
            P(("expert", "fsdp"), None),
            P(("expert", "fsdp"), None),
            P(("expert", "fsdp"), None),
            P(("expert", "fsdp"), None),
            P(("expert", "fsdp"), None),
            P("expert", None, "fsdp"),
            P("expert", None, "fsdp"),
            P("expert", None, "fsdp"),
            P("expert", "fsdp", None),
            P("expert", "fsdp", None),
            P("expert", "fsdp", None),
            P(),
            P(),
            P(),
            P(),
            P(),
            P(),
            P(),
            P(),
            P(),
        ),
        check_vma=False,
    )
```

time: 404 us -> 226 us (0.56)
  waiting for transfers between devices: 190 us -> 41.3 us
  starting transfers between devices: 22.7 us -> 38 us
  blocking collectives: 52 us -> 38.6 us
  between operations: 15.2 us -> 2.11 us
  local copies, waits for them, and re-layouts: 46.2 us -> 34.4 us
  matrix products: 52.6 us -> 42.2 us
  other arithmetic: 23.5 us -> 28.5 us
    unnamed x10 -> x0, waiting for transfers between devices: 122 us -> none
    psum x1 -> x0, blocking collectives: 42.7 us -> none  [local(): lax.psum((router_grad, jnp.stack([gain_one_grad, gain_two_grad]), table_g...]
    all_to_all x0 -> x1, blocking collectives: none -> 38.6 us  [local(): lax.all_to_all(dispatched.reshape(n_expert, capacity, 2 * model_width), '...]
    all_to_all x4 -> x1, waiting for transfers between devices: 47.3 us -> 10.2 us  [local(): lax.all_to_all(summed.reshape(n_expert, capacity, 2 * model_width), 'expe...]
    ppermute x0 -> x31, starting transfers between devices: none -> 33.4 us  [the longest x20 31 us: bit_swap(): lax.ppermute(value, 'expert', tuple(((i, i ^ 1 << bit) for i in range(siz...]
    ppermute x0 -> x31, waiting for transfers between devices: none -> 31.1 us  [the longest x20 28.7 us: bit_swap(): lax.ppermute(value, 'expert', tuple(((i, i ^ 1 << bit) for i in range(siz...]
    all_to_all x4 -> x1, starting transfers between devices: 22.2 us -> 4.56 us  [local(): lax.all_to_all(summed.reshape(n_expert, capacity, 2 * model_width), 'expe...]
    all_gather x2 -> x0, waiting for transfers between devices: 13.3 us -> none  [the longest x1 13 us: local(): lax.all_gather(qkv_weight, 'fsdp', axis=0, tiled=True)]
  transfers between devices with their start and end apart: 11 -> 32, of which waited for: 10 -> 17; matrix products, arithmetic and copies ran while one was open for 18% -> 26% of each run, Pallas kernels for 0% -> 0%
where the time goes in v1:
time: 226 us; the launch traced here: 225 us
  matrix products  42.2 us (19%)
  waiting for transfers between devices  41.3 us (18%)
  blocking collectives  38.6 us (17%)
  starting transfers between devices  38 us (17%)
  local copies, waits for them, and re-layouts  34.4 us (15%)
  other arithmetic  28.5 us (13%)
    all_to_all x1, blocking collectives, local(): lax.all_to_all(dispatched.reshape(n_expert, capacity, 2 * model_width), '...  38.6 us
    ppermute x20, starting transfers between devices, bit_swap(): lax.ppermute(value, 'expert', tuple(((i, i ^ 1 << bit) for i in range(siz...  31 us
    ppermute x20, waiting for transfers between devices, bit_swap(): lax.ppermute(value, 'expert', tuple(((i, i ^ 1 << bit) for i in range(siz...  28.7 us
    unnamed x163, local copies, waits for them, and re-layouts  11.2 us
    all_to_all x1, waiting for transfers between devices, local(): lax.all_to_all(summed.reshape(n_expert, capacity, 2 * model_width), 'expe...  10.2 us
    dot_general x1, matrix products, local(): jnp.einsum('rh,rd->hd', activated, grad_in, preferred_element_type=jnp.fl...  9.12 us
    sub x5, other arithmetic, adam_step(): weight - rate * (moment_hat / (jnp.sqrt(square_hat) + ADAM_EPS) + decay *...  7.7 us
    dot_general x1, matrix products, local(): jnp.einsum('rd,rh->dh', expert_in, pre_grad, preferred_element_type=jnp.f...  5.65 us
  transfers between devices with their start and end apart: 32, of which 17 were waited for; matrix products, arithmetic and copies ran while one was open for 26% of the time, Pallas kernels for 0%

profile of v1, /device:TPU:0, one launch (start us, length us, event | category | flops | bytes accessed | tf_op | source)
XLA Modules:
  0.0 225.1 jit_solution(18369581277791072532)
XLA Ops:
  4.2 2.0 fusion.121
  9.7 1.6 copy.91
  13.6 2.0 pad_maximum_fusion.3
  15.8 1.6 fusion.181
  18.0 1.2 copy.88
  20.1 1.5 multiply_reduce_fusion.3
  23.9 1.5 convolution_convert_fusion
  25.4 2.1 reshape.386
  27.5 38.6 %all_to_all.10 = bf16[16,20,1536]{2,1,0:T(8,128)(2,1)} all-to-all(bf16[16,20,1536]{2,1,0:T(8,128)(2,1)} %reshape.386), channel_id=1, replica_groups=mesh['expert'=16,'fsdp'=2] {'expert'}, dimensions={0} | all-to-all | bytes 1966080 | tf_op jit(solution)/shard_map/all_to_all | solution.py:223
  66.1 2.1 reshape.387
  68.3 1.4 constant_dynamic-update-slice_fusion.1
  69.6 1.4 collective-permute-done.3
  73.2 1.4 fusion.18
  76.8 1.2 fusion.22
  81.3 3.0 %fusion.21 = bf16[320,1536]{1,0:T(8,128)(2,1)} fusion(f32[640,768]{1,0:T(8,128)} %copy-done.1, f32[640,768]{1,0:T(8,128)} %copy-done, bf16[320,1536]{1,0:T(8,128)(2,1)} %collective-permute-done.4), kind=kLoop, calls=%fused_computation.35 | loop fusion | flops 1966080 | bytes 5898240 | tf_op jit(solution)/shard_map/convert_element_type | solution.py:247
  84.3 2.2 reshape.388
  86.5 4.6 %all-to-all-start.1 = ((bf16[16,20,1536]{2,1,0:T(8,128)(2,1)}), bf16[16,20,1536]{2,1,0:T(8,128)(2,1)}, u32[]{:S(2)}, u32[]{:S(2)}) async-start(bf16[16,20,1536]{2,1,0:T(8,128)(2,1)} %reshape.388), calls=%async_computation.1 | async-start | bytes 2359296 | tf_op jit(solution)/shard_map/all_to_all | solution.py:248
  93.0 9.1 %convert_subtract_fusion = (f32[1,768,768]{2,1,0:T(8,128)}, f32[1,768,768]{2,1,0:T(8,128)}, f32[1,768,768]{2,1,0:T(8,128)}) fusion(bf16[1,768,768]{2,1,0:T(8,128)(2,1)} %param.36, f32[1,768,768]{2,1,0:T(8,128)} %param.38, f32[1,768,768]{2,1,0:T(8,128)} %param.37, bf16[640,768]{1,0:T(8,128)(2,1)} %copy-done.78, bf16[640,1536]{1,0:T(8,128)(2,1)} %copy-done.29), kind=kOutput, calls=%fused_computation.9 | convolution fusion | flops 764411904 | bytes 14942208 | tf_op jit(solution)/shard_map/rh,rd->hd/dot_general | solution.py:256
  102.1 5.7 %convert_subtract_fusion.1 = (f32[1,768,768]{2,1,0:T(8,128)}, f32[1,768,768]{2,1,0:T(8,128)}, f32[1,768,768]{2,1,0:T(8,128)}) fusion(bf16[1,768,768]{2,1,0:T(8,128)(2,1)S(1)} %copy-done.75, f32[1,768,768]{2,1,0:T(8,128)S(1)} %copy-done.71, f32[1,768,768]{2,1,0:T(8,128)S(1)} %copy-done.72, bf16[640,768]{1,0:T(8,128)(2,1)S(1)} %copy-done.77, ...), kind=kOutput, calls=%fused_computation.11 | convolution fusion | flops 764411904 | bytes 14942208 | tf_op jit(solution)/shard_map/rd,rh->dh/dot_general | solution.py:255
  107.8 10.2 %all-to-all-done.1 = bf16[16,20,1536]{2,1,0:T(8,128)(2,1)} async-done(((bf16[16,20,1536]{2,1,0:T(8,128)(2,1)}), bf16[16,20,1536]{2,1,0:T(8,128)(2,1)}, u32[]{:S(2)}, u32[]{:S(2)}) %all-to-all-start.1) | async-done | bytes 983072 | tf_op jit(solution)/shard_map/all_to_all | solution.py:248
  118.0 2.1 reshape.389
  120.2 1.6 fusion.106
  124.4 2.0 convolution_convert_fusion.2
  126.4 1.1 copy.93
  127.5 1.4 fusion.93
  130.6 1.1 fusion.38
  132.0 1.8 copy.102
  133.8 2.0 fusion.39
  142.5 1.4 copy-done.20
  147.0 1.1 collective-permute-start.27
  148.1 3.1 %collective-permute-done.27 = f32[11,768]{1,0:T(8,128)S(1)} collective-permute-done((f32[11,768]{1,0:T(8,128)S(1)}, f32[11,768]{1,0:T(8,128)S(1)}, u32[]{:S(2)}, u32[]{:S(2)}) %collective-permute-start.27) | collective-permute-done | bytes 33824 | tf_op jit(solution)/shard_map/ppermute | solution.py:67
  151.2 2.2 collective-permute-start.28
  154.4 1.1 collective-permute-done.28
  155.5 3.7 %collective-permute-start.29 = (f32[11,768]{1,0:T(8,128)S(1)}, f32[11,768]{1,0:T(8,128)S(1)}, u32[]{:S(2)}, u32[]{:S(2)}) collective-permute-start(f32[11,768]{1,0:T(8,128)S(1)} %add.491), channel_id=1, source_target_pairs={{0,8},{2,10},{4,12},{6,14},{8,0},{10,2},{12,4},{14,6},{16,24},{18,... | collective-permute-start | bytes 101384 | tf_op jit(solution)/shard_map/ppermute | solution.py:67
  159.3 1.9 collective-permute-done.29
  161.2 2.5 %collective-permute-start.30 = (f32[11,768]{1,0:T(8,128)S(1)}, f32[11,768]{1,0:T(8,128)S(1)}, u32[]{:S(2)}, u32[]{:S(2)}) collective-permute-start(f32[11,768]{1,0:T(8,128)S(1)} %add.492), channel_id=1, source_target_pairs={{0,16},{2,18},{4,20},{6,22},{8,24},{10,26},{12,28},{14,30},{16,0},... | collective-permute-start | bytes 101384 | tf_op jit(solution)/shard_map/ppermute | solution.py:67
  163.9 2.4 %collective-permute-done.30 = f32[11,768]{1,0:T(8,128)S(1)} collective-permute-done((f32[11,768]{1,0:T(8,128)S(1)}, f32[11,768]{1,0:T(8,128)S(1)}, u32[]{:S(2)}, u32[]{:S(2)}) %collective-permute-start.30) | collective-permute-done | bytes 33824 | tf_op jit(solution)/shard_map/ppermute | solution.py:67
  167.6 1.4 copy.104
  169.0 1.4 convert_subtract_fusion.4
  170.4 1.4 convert_subtract_fusion.2
  171.8 1.4 convert_subtract_fusion.3
  173.2 1.6 bitcast_add_fusion.3
  174.8 2.1 collective-permute-start.22
  176.9 1.2 bitcast_add_fusion.6
  178.1 1.2 collective-permute-start.7
  179.3 3.3 %collective-permute-done.22 = bf16[2,2,2,24,768]{4,3,2,1,0:T(8,128)(2,1)S(1)} collective-permute-done((bf16[2,2,2,24,768]{4,3,2,1,0:T(8,128)(2,1)S(1)}, bf16[2,2,2,24,768]{4,3,2,1,0:T(8,128)(2,1)S(1)}, u32[]{:S(2)}, u32[]{:S(2)}) %collective-permute-start.22) | collective-permute-done | bytes 294944 | tf_op jit(solution)/shard_map/ppermute | solution.py:67
  182.7 2.5 %collective-permute-start.23 = (bf16[2,2,24,768]{3,2,1,0:T(8,128)(2,1)S(1)}, bf16[2,2,24,768]{3,2,1,0:T(8,128)(2,1)S(1)}, u32[]{:S(2)}, u32[]{:S(2)}) collective-permute-start(bf16[2,2,24,768]{3,2,1,0:T(8,128)(2,1)S(1)} %fusion.110), channel_id=1, source_target_pairs={{0,16},{2,18},{4,20},{6,22},{8,24},{10,26},{12,28},{14,30},{16,0},... | collective-permute-start | bytes 442376 | tf_op jit(solution)/shard_map/ppermute | solution.py:67
  185.3 1.1 collective-permute-start.8
  186.4 1.2 bitcast_add_fusion.4
  187.7 1.4 collective-permute-start.17
  189.1 1.2 bitcast_add_fusion.5
  190.6 1.3 collective-permute-start.24
  192.2 1.9 collective-permute-start.9
  195.1 1.9 collective-permute-start.25
  197.1 2.1 collective-permute-start.10
  199.3 1.2 multiply_subtract_fusion.1
  200.5 2.0 collective-permute-done.10
  202.6 1.8 collective-permute-start.18
  205.4 5.7 %collective-permute-done.18 = bf16[2,2,24,768]{3,2,0,1:T(8,128)(2,1)S(1)} collective-permute-done((bf16[2,2,24,768]{3,2,0,1:T(8,128)(2,1)S(1)}, bf16[2,2,24,768]{3,2,0,1:T(8,128)(2,1)S(1)}, u32[]{:S(2)}, u32[]{:S(2)}) %collective-permute-start.18) | collective-permute-done | bytes 147488 | tf_op jit(solution)/shard_map/ppermute | solution.py:67
  211.1 1.9 collective-permute-start.19
  213.1 2.4 %collective-permute-done.19 = bf16[2,24,768]{2,1,0:T(8,128)(2,1)S(1)} collective-permute-done((bf16[2,24,768]{2,1,0:T(8,128)(2,1)S(1)}, bf16[2,24,768]{2,1,0:T(8,128)(2,1)S(1)}, u32[]{:S(2)}, u32[]{:S(2)}) %collective-permute-start.19) | collective-permute-done | bytes 73760 | tf_op jit(solution)/shard_map/ppermute | solution.py:67
  216.5 1.9 collective-permute-done.14
  219.6 2.8 %collective-permute-done.15 = bf16[24,768]{1,0:T(8,128)(2,1)S(1)} collective-permute-done((bf16[24,768]{1,0:T(8,128)(2,1)S(1)}, bf16[24,768]{1,0:T(8,128)(2,1)S(1)}, u32[]{:S(2)}, u32[]{:S(2)}) %collective-permute-start.15) | collective-permute-done | bytes 36896 | tf_op jit(solution)/shard_map/ppermute | solution.py:67
  222.7 2.4 %multiply_subtract_fusion = (f32[1,55296]{1,0:T(1,128)}, f32[1,55296]{1,0:T(1,128)}, f32[1,55296]{1,0:T(1,128)}) fusion(f32[1,55296]{1,0:T(1,128)S(1)} %bitcast.240, f32[1,55296]{1,0:T(1,128)S(1)} %bitcast.241, f32[1,55296]{1,0:T(1,128)S(1)} %copy-done.32, f32[1,55296]{1,0:T(1,128)S(1)} %copy-done.33), kind=kLoop, calls=%fused_computation.171 | loop fusion | flops 829440 | bytes 1548288 | tf_op jit(solution)/shard_map/sub | solution.py:57
  (300 shorter events, 44.9 us)
Async XLA Ops:
  0.7 5.6 %collective-permute-start = (bf16[384,2304]{1,0:T(8,128)(2,1)}, bf16[384,2304]{1,0:T(8,128)(2,1)S(1)}, u32[]{:S(2)}, u32[]{:S(2)}) collective-permute-start(bf16[384,2304]{1,0:T(8,128)(2,1)} %param.27), channel_id=1, source_target_pairs={{0,1},{1,0},{2,3},{3,2},{4,5},{5,4},{6,7},{7,6},{8,9},{9,8},{10,11... | collective-permute-start | bytes 5308424 | tf_op jit(solution)/shard_map/ppermute | solution.py:62
  1.2 18.9 %collective-permute-start.2 = (bf16[384,768]{1,0:T(8,128)(2,1)}, bf16[384,768]{1,0:T(8,128)(2,1)}, u32[]{:S(2)}, u32[]{:S(2)}) collective-permute-start(bf16[384,768]{1,0:T(8,128)(2,1)} %param.30), channel_id=1, source_target_pairs={{0,1},{1,0},{2,3},{3,2},{4,5},{5,4},{6,7},{7,6},{8,9},{9,8},{10,11... | collective-permute-start | bytes 1769480 | tf_op jit(solution)/shard_map/ppermute | solution.py:62
  3.1 3.6 %copy-start.59 = (f32[128]{0:T(128)}, f32[128]{0:T(128)S(1)}, u32[]{:S(2)}) copy-start(f32[128]{0:T(128)S(1)} %add_rsqrt_fusion.1) | copy-start | bytes 1540
  7.6 6.0 %collective-permute-start.1 = (bf16[128,1536]{1,0:T(8,128)(2,1)}, bf16[128,1536]{1,0:T(8,128)(2,1)}, u32[]{:S(2)}, u32[]{:S(2)}) collective-permute-start(bf16[128,1536]{1,0:T(8,128)(2,1)} %slice.78), channel_id=1, source_target_pairs={{0,1},{1,0},{2,3},{3,2},{4,5},{5,4},{6,7},{7,6},{8,9},{9,8},{10,11... | collective-permute-start | bytes 1179656 | tf_op jit(solution)/shard_map/ppermute | solution.py:62
  11.3 4.6 %copy-start.11 = (f32[128,256,12]{1,0,2:T(8,128)S(1)}, f32[128,256,12]{1,0,2:T(8,128)}, u32[]{:S(2)}) copy-start(f32[128,256,12]{1,0,2:T(8,128)} %copy.91) | copy-start | bytes 4718596
  19.7 3.5 %copy-start.50 = (s32[128]{0:T(128)S(1)}, s32[128]{0:T(128)}, u32[]{:S(2)}) copy-start(s32[128]{0:T(128)} %param.48) | copy-start | bytes 1540
  19.7 4.1 %copy-start.24 = (bf16[128,768]{1,0:T(8,128)(2,1)S(1)}, bf16[128,768]{1,0:T(8,128)(2,1)}, u32[]{:S(2)}) copy-start(bf16[128,768]{1,0:T(8,128)(2,1)} %param.26) | copy-start | bytes 589828
  19.7 4.1 %copy-start.43 = (s32[320]{0:T(512)S(1)}, s32[320]{0:T(512)}, u32[]{:S(2)}) copy-start(s32[320]{0:T(512)} %get-tuple-element.88) | copy-start | bytes 3844
  19.8 4.1 %copy-start.45 = (s32[320]{0:T(512)S(1)}, s32[320]{0:T(512)}, u32[]{:S(2)}) copy-start(s32[320]{0:T(512)} %get-tuple-element.89) | copy-start | bytes 3844
  19.8 4.1 %copy-start.67 = (s32[128]{0:T(128)S(1)}, s32[128]{0:T(128)}, u32[]{:S(2)}) copy-start(s32[128]{0:T(128)} %param.49) | copy-start | bytes 1540
  68.3 2.9 %copy-start.74 = (bf16[1,768,768]{2,1,0:T(8,128)(2,1)S(1)}, bf16[1,768,768]{2,1,0:T(8,128)(2,1)}, u32[]{:S(2)}) copy-start(bf16[1,768,768]{2,1,0:T(8,128)(2,1)} %param.33) | copy-start | bytes 3538948
  68.3 2.8 %collective-permute-start.3 = (bf16[320,1536]{1,0:T(8,128)(2,1)}, bf16[320,1536]{1,0:T(8,128)(2,1)S(1)}, u32[]{:S(2)}, u32[]{:S(2)}) collective-permute-start(bf16[320,1536]{1,0:T(8,128)(2,1)} %reshape.387), channel_id=1, source_target_pairs={{0,1},{1,0},{2,3},{3,2},{4,5},{5,4},{6,7},{7,6},{8,9},{9,8},{10,11... | collective-permute-start | bytes 2949128 | tf_op jit(solution)/shard_map/ppermute | solution.py:62
  72.1 3.4 %copy-start.78 = (bf16[640,768]{1,0:T(8,128)(2,1)}, bf16[640,768]{1,0:T(8,128)(2,1)S(1)}, u32[]{:S(2)}) copy-start(bf16[640,768]{1,0:T(8,128)(2,1)S(1)} %get-tuple-element.83) | copy-start | bytes 2949124
  78.4 2.9 %collective-permute-start.4 = (bf16[320,1536]{1,0:T(8,128)(2,1)}, bf16[320,1536]{1,0:T(8,128)(2,1)}, u32[]{:S(2)}, u32[]{:S(2)}) collective-permute-start(bf16[320,1536]{1,0:T(8,128)(2,1)} %fusion.22), channel_id=1, source_target_pairs={{0,1},{1,0},{2,3},{3,2},{4,5},{5,4},{6,7},{7,6},{8,9},{9,8},{10,11... | collective-permute-start | bytes 2949128 | tf_op jit(solution)/shard_map/ppermute | solution.py:62
  86.5 31.5 %all-to-all-start.1 = ((bf16[16,20,1536]{2,1,0:T(8,128)(2,1)}), bf16[16,20,1536]{2,1,0:T(8,128)(2,1)}, u32[]{:S(2)}, u32[]{:S(2)}) async-start(bf16[16,20,1536]{2,1,0:T(8,128)(2,1)} %reshape.388), calls=%async_computation.1 | async-start | bytes 2359296 | tf_op jit(solution)/shard_map/all_to_all | solution.py:248
  92.9 9.1 %copy-start.30 = (bf16[640,1536]{1,0:T(8,128)(2,1)S(1)}, bf16[640,1536]{1,0:T(8,128)(2,1)}, u32[]{:S(2)}) copy-start(bf16[640,1536]{1,0:T(8,128)(2,1)} %copy-done.29) | copy-start | bytes 5898244
  92.9 9.1 %copy-start.71 = (f32[1,768,768]{2,1,0:T(8,128)S(1)}, f32[1,768,768]{2,1,0:T(8,128)}, u32[]{:S(2)}) copy-start(f32[1,768,768]{2,1,0:T(8,128)} %param.35) | copy-start | bytes 7077892
  92.9 9.1 %copy-start.72 = (f32[1,768,768]{2,1,0:T(8,128)S(1)}, f32[1,768,768]{2,1,0:T(8,128)}, u32[]{:S(2)}) copy-start(f32[1,768,768]{2,1,0:T(8,128)} %param.34) | copy-start | bytes 7077892
  92.9 9.1 %copy-start.75 = (bf16[1,768,768]{2,1,0:T(8,128)(2,1)S(1)}, bf16[1,768,768]{2,1,0:T(8,128)(2,1)}, u32[]{:S(2)}) copy-start(bf16[1,768,768]{2,1,0:T(8,128)(2,1)} %param.33) | copy-start | bytes 3538948
  92.9 9.2 %copy-start.77 = (bf16[640,768]{1,0:T(8,128)(2,1)S(1)}, bf16[640,768]{1,0:T(8,128)(2,1)}, u32[]{:S(2)}) copy-start(bf16[640,768]{1,0:T(8,128)(2,1)} %copy-done.76) | copy-start | bytes 2949124
  107.8 12.4 %copy-start.44 = (s32[320]{0:T(512)S(1)}, s32[320]{0:T(512)}, u32[]{:S(2)}) copy-start(s32[320]{0:T(512)} %get-tuple-element.88) | copy-start | bytes 3844
  107.8 12.4 %copy-start.46 = (s32[320]{0:T(512)S(1)}, s32[320]{0:T(512)}, u32[]{:S(2)}) copy-start(s32[320]{0:T(512)} %get-tuple-element.89) | copy-start | bytes 3844
  107.8 12.4 %copy-start.51 = (s32[128]{0:T(128)S(1)}, s32[128]{0:T(128)}, u32[]{:S(2)}) copy-start(s32[128]{0:T(128)} %param.48) | copy-start | bytes 1540
  107.8 12.4 %copy-start.68 = (s32[128]{0:T(128)S(1)}, s32[128]{0:T(128)}, u32[]{:S(2)}) copy-start(s32[128]{0:T(128)} %param.49) | copy-start | bytes 1540
  107.8 14.1 %copy-start.66 = (f32[128]{0:T(128)S(1)}, f32[128]{0:T(128)}, u32[]{:S(2)}) copy-start(f32[128]{0:T(128)} %copy-done.65) | copy-start | bytes 1540
  132.0 4.5 %copy-start.10 = (f32[12,64,256]{2,1,0:T(8,128)S(1)}, f32[12,64,256]{2,1,0:T(8,128)}, u32[]{:S(2)}) copy-start(f32[12,64,256]{2,1,0:T(8,128)} %fusion.93) | copy-start | bytes 2359300
  136.5 4.6 %collective-permute-start.5 = (bf16[128,1536]{0,1:T(8,128)(2,1)S(1)}, bf16[128,1536]{0,1:T(8,128)(2,1)S(1)}, u32[]{:S(2)}, u32[]{:S(2)}) collective-permute-start(bf16[128,1536]{0,1:T(8,128)(2,1)S(1)} %fusion.49), channel_id=1, source_target_pairs={{0,1},{1,0},{2,3},{3,2},{4,5},{5,4},{6,7},{7,6},{8,9},{9,8},{10,11... | collective-permute-start | bytes 1179656 | tf_op jit(solution)/shard_map/ppermute | solution.py:62
  138.0 35.1 %collective-permute-start.21 = (bf16[16,24,768]{2,1,0:T(8,128)(2,1)}, bf16[16,24,768]{2,1,0:T(8,128)(2,1)}, u32[]{:S(2)}, u32[]{:S(2)}) collective-permute-start(bf16[16,24,768]{2,1,0:T(8,128)(2,1)} %fusion.55), channel_id=1, source_target_pairs={{0,1},{1,0},{2,3},{3,2},{4,5},{5,4},{6,7},{7,6},{8,9},{9,8},{10,11... | collective-permute-start | bytes 1769480 | tf_op jit(solution)/shard_map/ppermute | solution.py:62
  140.1 36.7 %collective-permute-start.6 = (bf16[16,24,768]{2,1,0:T(8,128)(2,1)}, bf16[16,24,768]{2,1,0:T(8,128)(2,1)}, u32[]{:S(2)}, u32[]{:S(2)}) collective-permute-start(bf16[16,24,768]{2,1,0:T(8,128)(2,1)} %fusion.54), channel_id=1, source_target_pairs={{0,1},{1,0},{2,3},{3,2},{4,5},{5,4},{6,7},{7,6},{8,9},{9,8},{10,11... | collective-permute-start | bytes 1769480 | tf_op jit(solution)/shard_map/ppermute | solution.py:62
  141.7 17.5 %copy-start.2 = (f32[768,768]{1,0:T(8,128)}, f32[768,768]{1,0:T(8,128)S(1)}, u32[]{:S(2)}) copy-start(f32[768,768]{1,0:T(8,128)S(1)} %fusion.96) | copy-start | bytes 7077892
  145.7 1.3 collective-permute-start.26
  146.3 17.5 %copy-start.4 = (f32[768,768]{1,0:T(8,128)}, f32[768,768]{1,0:T(8,128)S(1)}, u32[]{:S(2)}) copy-start(f32[768,768]{1,0:T(8,128)S(1)} %fusion.98) | copy-start | bytes 7077892
  147.0 4.2 %collective-permute-start.27 = (f32[11,768]{1,0:T(8,128)S(1)}, f32[11,768]{1,0:T(8,128)S(1)}, u32[]{:S(2)}, u32[]{:S(2)}) collective-permute-start(f32[11,768]{1,0:T(8,128)S(1)} %fusion.173), channel_id=1, source_target_pairs={{0,2},{2,0},{4,6},{6,4},{8,10},{10,8},{12,14},{14,12},{16,18},{18,... | collective-permute-start | bytes 101384 | tf_op jit(solution)/shard_map/ppermute | solution.py:67
  151.2 19.2 %copy-start.37 = (bf16[768,8]{0,1:T(8,128)(2,1)S(1)}, bf16[768,8]{0,1:T(8,128)(2,1)}, u32[]{:S(2)}) copy-start(bf16[768,8]{0,1:T(8,128)(2,1)} %param.39) | copy-start | bytes 36868
  151.2 4.3 %collective-permute-start.28 = (f32[11,768]{1,0:T(8,128)S(1)}, f32[11,768]{1,0:T(8,128)S(1)}, u32[]{:S(2)}, u32[]{:S(2)}) collective-permute-start(f32[11,768]{1,0:T(8,128)S(1)} %add.490), channel_id=1, source_target_pairs={{0,4},{2,6},{4,0},{6,2},{8,12},{10,14},{12,8},{14,10},{16,20},{18,... | collective-permute-start | bytes 101384 | tf_op jit(solution)/shard_map/ppermute | solution.py:67
  155.5 5.7 %collective-permute-start.29 = (f32[11,768]{1,0:T(8,128)S(1)}, f32[11,768]{1,0:T(8,128)S(1)}, u32[]{:S(2)}, u32[]{:S(2)}) collective-permute-start(f32[11,768]{1,0:T(8,128)S(1)} %add.491), channel_id=1, source_target_pairs={{0,8},{2,10},{4,12},{6,14},{8,0},{10,2},{12,4},{14,6},{16,24},{18,... | collective-permute-start | bytes 101384 | tf_op jit(solution)/shard_map/ppermute | solution.py:67
  159.2 27.2 %collective-permute-start.16 = (bf16[16,24,768]{2,1,0:T(8,128)(2,1)S(1)}, bf16[16,24,768]{2,1,0:T(8,128)(2,1)}, u32[]{:S(2)}, u32[]{:S(2)}) collective-permute-start(bf16[16,24,768]{2,1,0:T(8,128)(2,1)S(1)} %fusion.56), channel_id=1, source_target_pairs={{0,1},{1,0},{2,3},{3,2},{4,5},{5,4},{6,7},{7,6},{8,9},{9,8},{10,11... | collective-permute-start | bytes 1769480 | tf_op jit(solution)/shard_map/ppermute | solution.py:62
  161.2 5.0 %collective-permute-start.30 = (f32[11,768]{1,0:T(8,128)S(1)}, f32[11,768]{1,0:T(8,128)S(1)}, u32[]{:S(2)}, u32[]{:S(2)}) collective-permute-start(f32[11,768]{1,0:T(8,128)S(1)} %add.492), channel_id=1, source_target_pairs={{0,16},{2,18},{4,20},{6,22},{8,24},{10,26},{12,28},{14,30},{16,0},... | collective-permute-start | bytes 101384 | tf_op jit(solution)/shard_map/ppermute | solution.py:67
  163.8 13.1 %copy-start.7 = (f32[16,2,24,768]{3,2,1,0:T(8,128)S(1)}, f32[16,2,24,768]{3,2,1,0:T(8,128)}, u32[]{:S(2)}) copy-start(f32[16,2,24,768]{3,2,1,0:T(8,128)} %copy-done.6) | copy-start | bytes 7077892
  163.8 25.3 %collective-permute-start.11 = (bf16[16,24,768]{2,1,0:T(8,128)(2,1)S(1)}, bf16[16,24,768]{2,1,0:T(8,128)(2,1)}, u32[]{:S(2)}, u32[]{:S(2)}) collective-permute-start(bf16[16,24,768]{2,1,0:T(8,128)(2,1)S(1)} %fusion.57), channel_id=1, source_target_pairs={{0,1},{1,0},{2,3},{3,2},{4,5},{5,4},{6,7},{7,6},{8,9},{9,8},{10,11... | collective-permute-start | bytes 1769480 | tf_op jit(solution)/shard_map/ppermute | solution.py:62
  174.8 7.8 %collective-permute-start.22 = (bf16[2,2,2,24,768]{4,3,2,1,0:T(8,128)(2,1)S(1)}, bf16[2,2,2,24,768]{4,3,2,1,0:T(8,128)(2,1)S(1)}, u32[]{:S(2)}, u32[]{:S(2)}) collective-permute-start(bf16[2,2,2,24,768]{4,3,2,1,0:T(8,128)(2,1)S(1)} %fusion.80), channel_id=1, source_target_pairs={{0,8},{2,10},{4,12},{6,14},{8,0},{10,2},{12,4},{14,6},{16,24},{18,... | collective-permute-start | bytes 884744 | tf_op jit(solution)/shard_map/ppermute | solution.py:67
  178.1 8.4 %copy-start.3 = (f32[768,768]{1,0:T(8,128)S(1)}, f32[768,768]{1,0:T(8,128)}, u32[]{:S(2)}) copy-start(f32[768,768]{1,0:T(8,128)} %copy-done.2) | copy-start | bytes 7077892
  178.1 7.1 %collective-permute-start.7 = (bf16[2,2,2,24,768]{4,3,0,1,2:T(8,128)(2,1)S(1)}, bf16[2,2,2,24,768]{4,3,0,1,2:T(8,128)(2,1)S(1)}, u32[]{:S(2)}, u32[]{:S(2)}) collective-permute-start(bf16[2,2,2,24,768]{4,3,0,1,2:T(8,128)(2,1)S(1)} %fusion.81), channel_id=1, source_target_pairs={{0,2},{2,0},{4,6},{6,4},{8,10},{10,8},{12,14},{14,12},{16,18},{18,... | collective-permute-start | bytes 884744 | tf_op jit(solution)/shard_map/ppermute | solution.py:67
  182.7 7.9 %collective-permute-start.23 = (bf16[2,2,24,768]{3,2,1,0:T(8,128)(2,1)S(1)}, bf16[2,2,24,768]{3,2,1,0:T(8,128)(2,1)S(1)}, u32[]{:S(2)}, u32[]{:S(2)}) collective-permute-start(bf16[2,2,24,768]{3,2,1,0:T(8,128)(2,1)S(1)} %fusion.110), channel_id=1, source_target_pairs={{0,16},{2,18},{4,20},{6,22},{8,24},{10,26},{12,28},{14,30},{16,0},... | collective-permute-start | bytes 442376 | tf_op jit(solution)/shard_map/ppermute | solution.py:67
  185.3 3.8 %copy-start.5 = (f32[768,768]{1,0:T(8,128)S(1)}, f32[768,768]{1,0:T(8,128)}, u32[]{:S(2)}) copy-start(f32[768,768]{1,0:T(8,128)} %copy-done.4) | copy-start | bytes 7077892
  185.3 6.8 %collective-permute-start.8 = (bf16[2,2,24,768]{3,2,0,1:T(8,128)(2,1)S(1)}, bf16[2,2,24,768]{3,2,0,1:T(8,128)(2,1)S(1)}, u32[]{:S(2)}, u32[]{:S(2)}) collective-permute-start(bf16[2,2,24,768]{3,2,0,1:T(8,128)(2,1)S(1)} %fusion.107), channel_id=1, source_target_pairs={{0,4},{2,6},{4,0},{6,2},{8,12},{10,14},{12,8},{14,10},{16,20},{18,... | collective-permute-start | bytes 442376 | tf_op jit(solution)/shard_map/ppermute | solution.py:67
  187.7 14.8 %collective-permute-start.17 = (bf16[2,2,2,24,768]{4,3,1,2,0:T(8,128)(2,1)S(1)}, bf16[2,2,2,24,768]{4,3,1,2,0:T(8,128)(2,1)S(1)}, u32[]{:S(2)}, u32[]{:S(2)}) collective-permute-start(bf16[2,2,2,24,768]{4,3,1,2,0:T(8,128)(2,1)S(1)} %fusion.82), channel_id=1, source_target_pairs={{0,8},{2,10},{4,12},{6,14},{8,0},{10,2},{12,4},{14,6},{16,24},{18,... | collective-permute-start | bytes 884744 | tf_op jit(solution)/shard_map/ppermute | solution.py:67
  190.2 9.0 %copy-start.31 = (f32[1,1,24,768]{3,1,2,0:T(1,128)S(1)}, f32[1,1,24,768]{3,1,2,0:T(1,128)}, u32[]{:S(2)}) copy-start(f32[1,1,24,768]{3,1,2,0:T(1,128)} %copy.119) | copy-start | bytes 221188
  190.3 9.0 %copy-start.41 = (f32[1,18432]{1,0:T(1,128)S(1)}, f32[1,18432]{1,0:T(1,128)}, u32[]{:S(2)}) copy-start(f32[1,18432]{1,0:T(1,128)} %param.32) | copy-start | bytes 221188
  190.3 9.0 %copy-start.42 = (f32[1,18432]{1,0:T(1,128)S(1)}, f32[1,18432]{1,0:T(1,128)}, u32[]{:S(2)}) copy-start(f32[1,18432]{1,0:T(1,128)} %param.31) | copy-start | bytes 221188
  190.3 14.0 %collective-permute-start.12 = (bf16[2,2,2,24,768]{4,3,2,1,0:T(8,128)(2,1)S(1)}, bf16[2,2,2,24,768]{4,3,2,1,0:T(8,128)(2,1)S(1)}, u32[]{:S(2)}, u32[]{:S(2)}) collective-permute-start(bf16[2,2,2,24,768]{4,3,2,1,0:T(8,128)(2,1)S(1)} %fusion.79), channel_id=1, source_target_pairs={{0,4},{2,6},{4,0},{6,2},{8,12},{10,14},{12,8},{14,10},{16,20},{18,... | collective-permute-start | bytes 884744 | tf_op jit(solution)/shard_map/ppermute | solution.py:67
  190.6 4.4 %collective-permute-start.24 = (bf16[2,24,768]{2,1,0:T(8,128)(2,1)S(1)}, bf16[2,24,768]{2,1,0:T(8,128)(2,1)S(1)}, u32[]{:S(2)}, u32[]{:S(2)}) collective-permute-start(bf16[2,24,768]{2,1,0:T(8,128)(2,1)S(1)} %fusion.131), channel_id=1, source_target_pairs={{0,2},{2,0},{4,6},{6,4},{8,10},{10,8},{12,14},{14,12},{16,18},{18,... | collective-permute-start | bytes 221192 | tf_op jit(solution)/shard_map/ppermute | solution.py:67
  192.2 4.8 %collective-permute-start.9 = (bf16[2,24,768]{2,1,0:T(8,128)(2,1)S(1)}, bf16[2,24,768]{2,1,0:T(8,128)(2,1)S(1)}, u32[]{:S(2)}, u32[]{:S(2)}) collective-permute-start(bf16[2,24,768]{2,1,0:T(8,128)(2,1)S(1)} %fusion.128), channel_id=1, source_target_pairs={{0,8},{2,10},{4,12},{6,14},{8,0},{10,2},{12,4},{14,6},{16,24},{18,... | collective-permute-start | bytes 221192 | tf_op jit(solution)/shard_map/ppermute | solution.py:67
  195.1 4.1 %collective-permute-start.25 = (bf16[24,768]{1,0:T(8,128)(2,1)S(1)}, bf16[24,768]{1,0:T(8,128)(2,1)S(1)}, u32[]{:S(2)}, u32[]{:S(2)}) collective-permute-start(bf16[24,768]{1,0:T(8,128)(2,1)S(1)} %fusion.136), channel_id=1, source_target_pairs={{0,4},{2,6},{4,0},{6,2},{8,12},{10,14},{12,8},{14,10},{16,20},{18,... | collective-permute-start | bytes 110600 | tf_op jit(solution)/shard_map/ppermute | solution.py:67
  197.1 5.4 %collective-permute-start.10 = (bf16[24,768]{1,0:T(8,128)(2,1)S(1)}, bf16[24,768]{1,0:T(8,128)(2,1)S(1)}, u32[]{:S(2)}, u32[]{:S(2)}) collective-permute-start(bf16[24,768]{1,0:T(8,128)(2,1)S(1)} %fusion.133), channel_id=1, source_target_pairs={{0,16},{2,18},{4,20},{6,22},{8,24},{10,26},{12,28},{14,30},{16,0},... | collective-permute-start | bytes 110600 | tf_op jit(solution)/shard_map/ppermute | solution.py:67
  202.6 8.5 %collective-permute-start.18 = (bf16[2,2,24,768]{3,2,0,1:T(8,128)(2,1)S(1)}, bf16[2,2,24,768]{3,2,0,1:T(8,128)(2,1)S(1)}, u32[]{:S(2)}, u32[]{:S(2)}) collective-permute-start(bf16[2,2,24,768]{3,2,0,1:T(8,128)(2,1)S(1)} %fusion.109), channel_id=1, source_target_pairs={{0,16},{2,18},{4,20},{6,22},{8,24},{10,26},{12,28},{14,30},{16,0},... | collective-permute-start | bytes 442376 | tf_op jit(solution)/shard_map/ppermute | solution.py:67
  204.5 18.2 %copy-start.25 = (f32[1,1,24,2304]{3,1,2,0:T(1,128)S(1)}, f32[1,1,24,2304]{3,1,2,0:T(1,128)}, u32[]{:S(2)}) copy-start(f32[1,1,24,2304]{3,1,2,0:T(1,128)} %copy.117) | copy-start | bytes 663556
  204.5 18.2 %copy-start.32 = (f32[1,55296]{1,0:T(1,128)S(1)}, f32[1,55296]{1,0:T(1,128)}, u32[]{:S(2)}) copy-start(f32[1,55296]{1,0:T(1,128)} %param.29) | copy-start | bytes 663556
  204.5 18.2 %copy-start.33 = (f32[1,55296]{1,0:T(1,128)S(1)}, f32[1,55296]{1,0:T(1,128)}, u32[]{:S(2)}) copy-start(f32[1,55296]{1,0:T(1,128)} %param.28) | copy-start | bytes 663556
  204.5 8.5 %collective-permute-start.13 = (bf16[2,2,24,768]{3,2,1,0:T(8,128)(2,1)S(1)}, bf16[2,2,24,768]{3,2,1,0:T(8,128)(2,1)S(1)}, u32[]{:S(2)}, u32[]{:S(2)}) collective-permute-start(bf16[2,2,24,768]{3,2,1,0:T(8,128)(2,1)S(1)} %fusion.108), channel_id=1, source_target_pairs={{0,8},{2,10},{4,12},{6,14},{8,0},{10,2},{12,4},{14,6},{16,24},{18,... | collective-permute-start | bytes 442376 | tf_op jit(solution)/shard_map/ppermute | solution.py:67
  211.1 4.4 %collective-permute-start.19 = (bf16[2,24,768]{2,1,0:T(8,128)(2,1)S(1)}, bf16[2,24,768]{2,1,0:T(8,128)(2,1)S(1)}, u32[]{:S(2)}, u32[]{:S(2)}) collective-permute-start(bf16[2,24,768]{2,1,0:T(8,128)(2,1)S(1)} %fusion.130), channel_id=1, source_target_pairs={{0,2},{2,0},{4,6},{6,4},{8,10},{10,8},{12,14},{14,12},{16,18},{18,... | collective-permute-start | bytes 221192 | tf_op jit(solution)/shard_map/ppermute | solution.py:67
  213.1 5.3 %collective-permute-start.14 = (bf16[2,24,768]{2,1,0:T(8,128)(2,1)S(1)}, bf16[2,24,768]{2,1,0:T(8,128)(2,1)S(1)}, u32[]{:S(2)}, u32[]{:S(2)}) collective-permute-start(bf16[2,24,768]{2,1,0:T(8,128)(2,1)S(1)} %fusion.129), channel_id=1, source_target_pairs={{0,16},{2,18},{4,20},{6,22},{8,24},{10,26},{12,28},{14,30},{16,0},... | collective-permute-start | bytes 221192 | tf_op jit(solution)/shard_map/ppermute | solution.py:67
  215.6 4.0 %collective-permute-start.20 = (bf16[24,768]{1,0:T(8,128)(2,1)S(1)}, bf16[24,768]{1,0:T(8,128)(2,1)S(1)}, u32[]{:S(2)}, u32[]{:S(2)}) collective-permute-start(bf16[24,768]{1,0:T(8,128)(2,1)S(1)} %fusion.135), channel_id=1, source_target_pairs={{0,4},{2,6},{4,0},{6,2},{8,12},{10,14},{12,8},{14,10},{16,20},{18,... | collective-permute-start | bytes 110600 | tf_op jit(solution)/shard_map/ppermute | solution.py:67
  218.4 4.0 %collective-permute-start.15 = (bf16[24,768]{1,0:T(8,128)(2,1)S(1)}, bf16[24,768]{1,0:T(8,128)(2,1)S(1)}, u32[]{:S(2)}, u32[]{:S(2)}) collective-permute-start(bf16[24,768]{1,0:T(8,128)(2,1)S(1)} %fusion.134), channel_id=1, source_target_pairs={{0,2},{2,0},{4,6},{6,4},{8,10},{10,8},{12,14},{14,12},{16,18},{18,... | collective-permute-start | bytes 110600 | tf_op jit(solution)/shard_map/ppermute | solution.py:67
  (47 other events, 79.1 us)

commit v2 on v1

--- a/solution.py
+++ b/solution.py
@@ -1,6 +1,11 @@
+import functools
+import itertools
+
 import jax
 import jax.numpy as jnp
 from jax import lax
+from jax.experimental import pallas as pl
+from jax.experimental.pallas import tpu as pltpu
 from jax.sharding import PartitionSpec as P
 
 FF = 3072
@@ -96,6 +101,158 @@
     for bit in range(bits):
         value = value + bit_swap(value, bit)
     return value
+
+
+def owner_sum_kernel(bits, orders, grad, small, total, small_total, held, *rest):
+    landed, (small_held, small_landed, send_sem, recv_sem, small_send, small_recv) = (
+        rest[: bits + 1],
+        rest[bits + 1 :],
+    )
+    pieces = len(orders)
+    core = lax.axis_index("fsdp")
+    place = lax.axis_index("expert")
+    mine = [lax.rem(lax.div(place, 1 << bit), 2) for bit in range(bits)]
+    partners = [{"fsdp": 1 - core}] + [
+        {"expert": place + (1 - 2 * mine[bit]) * (1 << bit)} for bit in range(bits)
+    ]
+
+    def mesh_copy(source, target, sent, received, partner):
+        return pltpu.make_async_remote_copy(
+            src_ref=source,
+            dst_ref=target,
+            send_sem=sent,
+            recv_sem=received,
+            device_id=partner,
+            device_id_type=pl.DeviceIdType.MESH,
+        )
+
+    barrier = pltpu.get_barrier_semaphore()
+    for partner in partners:
+        pl.semaphore_signal(
+            barrier, inc=1, device_id=partner, device_id_type=pl.DeviceIdType.MESH
+        )
+    pl.semaphore_wait(barrier, len(partners))
+
+    def piece_copy(piece, step):
+        sent, received = send_sem.at[piece, step], recv_sem.at[piece, step]
+        if step == 0:
+            return mesh_copy(
+                grad.at[1 - core, piece], landed[0].at[piece], sent, received, partners[0]
+            )
+        order = orders[piece]
+        place_of = [slice(None)] * bits
+        for bit in order[: step - 1]:
+            place_of[bits - 1 - bit] = mine[bit]
+        bit = order[step - 1]
+        place_of[bits - 1 - bit] = 1 - mine[bit]
+        return mesh_copy(
+            held.at[(piece, *place_of)],
+            landed[step].at[piece],
+            sent,
+            received,
+            partners[1 + bit],
+        )
+
+    def small_copy(step):
+        bit = step - 1
+        return mesh_copy(
+            small if step == 0 else small_held.at[step - 1],
+            small_landed.at[step],
+            small_send.at[step],
+            small_recv.at[step],
+            partners[1 + bit],
+        )
+
+    def add_part(piece, step, side):
+        order = orders[piece]
+        fixed = order[:step]
+        split = order[step] if step < bits else None
+        open_bits = [bit for bit in range(bits - 1, -1, -1) if bit not in fixed]
+        free_bits = [bit for bit in open_bits if bit != split]
+        for combo in itertools.product((0, 1), repeat=len(free_bits)):
+            values = dict(zip(free_bits, combo))
+            if split is not None:
+                values[split] = mine[split] if side else 1 - mine[split]
+            arrived_at = tuple(values[bit] for bit in open_bits)
+            for bit in fixed:
+                values[bit] = mine[bit]
+            held_at = tuple(values[bit] for bit in range(bits - 1, -1, -1))
+            arrived = landed[step][(piece, *arrived_at)].astype(jnp.float32)
+            if step == 0:
+                before = grad[(core, piece, *held_at)].astype(jnp.float32)
+            else:
+                before = held[(piece, *held_at)].astype(jnp.float32)
+            if split is None:
+                total[piece] = before + arrived
+            else:
+                held[(piece, *held_at)] = (before + arrived).astype(held.dtype)
+
+    for piece in range(pieces):
+        piece_copy(piece, 0).start()
+    small_copy(0).start()
+    for step in range(bits + 1):
+        for piece in range(pieces):
+            piece_copy(piece, step).wait_recv()
+            if step < bits:
+                add_part(piece, step, 0)
+                piece_copy(piece, step + 1).start()
+            add_part(piece, step, 1)
+        small_copy(step).wait_recv()
+        before = small[...] if step == 0 else small_held[step - 1]
+        if step < bits:
+            small_held[step] = before + small_landed[step]
+            small_copy(step + 1).start()
+        else:
+            small_total[...] = before + small_landed[step]
+    for step in range(bits + 1):
+        for piece in range(pieces):
+            piece_copy(piece, step).wait_send()
+        small_copy(step).wait_send()
+
+
+def owner_sum(grad, small):
+    n_expert = lax.axis_size("expert")
+    bits = n_expert.bit_length() - 1
+    rows, columns = grad.shape
+    block = rows // (2 * n_expert)
+    pieces = 3
+    width = columns // (2 * pieces)
+    order = list(range(bits))
+    orders = [order[shift:] + order[:shift] for shift in range(pieces)]
+    spread = (
+        grad.astype(jnp.bfloat16)
+        .reshape(n_expert, 2, block, pieces, 2, width)
+        .transpose(1, 3, 0, 4, 2, 5)
+        .reshape((2, pieces) + (2,) * bits + (2 * block, width))
+    )
+    vmem = pl.BlockSpec(memory_space=pltpu.VMEM)
+    slots = [
+        pltpu.VMEM((pieces,) + (2,) * (bits - step) + (2 * block, width), jnp.bfloat16)
+        for step in [0] + list(range(bits + 1))
+    ]
+    total, small_total = pl.pallas_call(
+        functools.partial(owner_sum_kernel, bits, orders),
+        out_shape=(
+            jax.ShapeDtypeStruct((pieces, 2 * block, width), jnp.float32),
+            jax.ShapeDtypeStruct(small.shape, jnp.float32),
+        ),
+        in_specs=[vmem, vmem],
+        out_specs=(vmem, vmem),
+        scratch_shapes=slots
+        + [
+            pltpu.VMEM((bits,) + small.shape, jnp.float32),
+            pltpu.VMEM((bits + 1,) + small.shape, jnp.float32),
+            pltpu.SemaphoreType.DMA((pieces, bits + 1)),
+            pltpu.SemaphoreType.DMA((pieces, bits + 1)),
+            pltpu.SemaphoreType.DMA((bits + 1,)),
+            pltpu.SemaphoreType.DMA((bits + 1,)),
+        ],
+        compiler_params=pltpu.CompilerParams(
+            collective_id=0, has_side_effects=True, vmem_limit_bytes=32 * 2**20
+        ),
+    )(spread, small)
+    total = total.reshape(pieces, 2, block, width).transpose(2, 0, 1, 3).reshape(block, columns)
+    return total, small_total
 
 
 def local(
@@ -311,15 +468,6 @@
             "td,te->de", normed_low, upstream_part, preferred_element_type=jnp.float32
         )
 
-    upward = list(range(bits))
-    out_sum = sum_to_owner(out_weight_grad, upward[2:] + upward[:2])
-    query_sum = sum_to_owner(weight_grad(query_grad), upward)
-    key_sum = sum_to_owner(
-        weight_grad(key_value_own[:, :model_width]), upward[1:] + upward[:1]
-    )
-    value_sum = sum_to_owner(
-        weight_grad(key_value_own[:, model_width:]), upward[2:] + upward[:2]
-    )
     normed_grad = times_transposed(qkv_grad, qkv_weight, qkv_other)
     input_part, gain_one_grad = norm_backward(inputs, inverse_one, gain_one, normed_grad)
     tokens_grad = middle_grad + input_part
@@ -333,12 +481,22 @@
         ],
         axis=0,
     )
-    small = sum_everywhere(small)
+    block = model_width // (n_expert * n_fsdp)
+    if block % 8 == 0:
+        small = jnp.pad(small, ((0, -small.shape[0] % 8), (0, 0)))
+        weight_sum, small = owner_sum(
+            jnp.concatenate([weight_grad(qkv_grad), out_weight_grad], axis=1), small
+        )
+        qkv_sum = weight_sum[:, : 3 * model_width].reshape(1, -1)
+        out_sum = weight_sum[:, 3 * model_width :].reshape(1, -1)
+    else:
+        upward = list(range(bits))
+        small = sum_everywhere(small)
+        qkv_sum = sum_to_owner(weight_grad(qkv_grad), upward).reshape(1, -1)
+        out_sum = sum_to_owner(out_weight_grad, upward[1:] + upward[:1]).reshape(1, -1)
     router_sum = small[:expert_count].T
     gain_sum = small[expert_count : expert_count + 2]
     table_sum = small[expert_count + 2, :table_size].reshape(bucket_count, head_count)
-    qkv_sum = jnp.concatenate([query_sum, key_sum, value_sum], axis=1).reshape(1, -1)
-    block = model_width // (n_expert * n_fsdp)
     first_row = own_index * block
     owner_core = first_row // half
     local_row = first_row - owner_core * half
@@ -351,7 +509,6 @@
 
     qkv_old = old_rows(qkv_weight, qkv_other)
     out_old = old_rows(out_weight, out_other)
-    out_sum = out_sum.reshape(1, -1)
     qkv_m, qkv_v, qkv_w = adam_step(
         qkv_old, qkv_moment, qkv_square, qkv_sum, 2.0 * model_width ** (-0.5), DECAY
     )

time: 226 us -> 208 us (0.920)
  Pallas kernels: 0 us -> 39.6 us
  starting transfers between devices: 38 us -> 5.73 us
  waiting for transfers between devices: 41.3 us -> 12.9 us
  local copies, waits for them, and re-layouts: 34.4 us -> 42.2 us
  other arithmetic: 28.5 us -> 24.1 us
    pallas_call x0 -> x1, Pallas kernels: none -> 39.6 us  [owner_sum(): pl.pallas_call(functools.partial(owner_sum_kernel, bits, orders), out_sha...]
    ppermute x20 -> x0, starting transfers between devices: 31 us -> none  [bit_swap(): lax.ppermute(value, 'expert', tuple(((i, i ^ 1 << bit) for i in range(siz...]
    ppermute x20 -> x0, waiting for transfers between devices: 28.7 us -> none  [bit_swap(): lax.ppermute(value, 'expert', tuple(((i, i ^ 1 << bit) for i in range(siz...]
    convert_element_type x20 -> x2, local copies, waits for them, and re-layouts: 2.41 us -> 15.3 us  [owner_sum(): grad.astype(jnp.bfloat16).reshape(n_expert, 2, block, pieces, 2, width)]
    add x24 -> x0, other arithmetic: 5.55 us -> none  [the longest x4 5.08 us: sum_to_owner(): total = kept + swap(sent.astype(jnp.bfloat16)).astype(jnp.float32)]
    dot_general x1, matrix products: 9.12 us -> 5.65 us  [local(): jnp.einsum('rh,rd->hd', activated, grad_in, preferred_element_type=jnp.fl...]
    dot_general x1, matrix products: 5.65 us -> 9.12 us  [local(): jnp.einsum('rd,rh->dh', expert_in, pre_grad, preferred_element_type=jnp.f...]
    concatenate x0 -> x1, other arithmetic: none -> 2.82 us  [local(): jnp.concatenate([weight_grad(qkv_grad), out_weight_grad], axis=1)]
  transfers between devices with their start and end apart: 32 -> 7, of which waited for: 17 -> 3; matrix products, arithmetic and copies ran while one was open for 26% -> 19% of each run, Pallas kernels for 0% -> 0%
where the time goes in v2:
time: 208 us; the launch traced here: 207 us
  local copies, waits for them, and re-layouts  42.2 us (20%)
  matrix products  42.1 us (20%)
  Pallas kernels  39.6 us (19%)
  blocking collectives  38.6 us (19%)
  other arithmetic  24.1 us (12%)
  waiting for transfers between devices  12.9 us (6%)
  starting transfers between devices  5.73 us (3%)
    pallas_call x1, Pallas kernels, owner_sum(): pl.pallas_call(functools.partial(owner_sum_kernel, bits, orders), out_sha...  39.6 us
    all_to_all x1, blocking collectives, local(): lax.all_to_all(dispatched.reshape(n_expert, capacity, 2 * model_width), '...  38.6 us
    convert_element_type x2, local copies, waits for them, and re-layouts, owner_sum(): grad.astype(jnp.bfloat16).reshape(n_expert, 2, block, pieces, 2, width)  15.3 us
    all_to_all x1, waiting for transfers between devices, local(): lax.all_to_all(summed.reshape(n_expert, capacity, 2 * model_width), 'expe...  10.2 us
    dot_general x1, matrix products, local(): jnp.einsum('rd,rh->dh', expert_in, pre_grad, preferred_element_type=jnp.f...  9.12 us
    unnamed x165, local copies, waits for them, and re-layouts  8.77 us
    dot_general x1, matrix products, local(): jnp.einsum('rh,rd->hd', activated, grad_in, preferred_element_type=jnp.fl...  5.65 us
    sub x5, other arithmetic, adam_step(): weight - rate * (moment_hat / (jnp.sqrt(square_hat) + ADAM_EPS) + decay *...  5.42 us
  transfers between devices with their start and end apart: 7, of which 3 were waited for; matrix products, arithmetic and copies ran while one was open for 19% of the time, Pallas kernels for 0%

profile of v2, /device:TPU:0, one launch (start us, length us, event | category | flops | bytes accessed | tf_op | source)
XLA Modules:
  0.0 207.1 jit_solution(15803963305669594974)
XLA Ops:
  1.3 0.8 convert_reduce_fusion
  2.1 1.0 fusion.64
  3.1 1.0 fusion.58
  4.2 2.0 fusion.103
  6.8 0.9 slice.78
  8.3 0.6 copy-done.20
  9.0 0.7 fusion.1
  9.7 1.6 copy.86
  11.9 0.8 copy.84
  12.7 2.0 pad_maximum_fusion.4
  14.9 1.6 fusion.156
  17.1 1.2 copy.83
  19.2 1.5 multiply_reduce_fusion.3
  22.9 1.5 convolution_convert_fusion.1
  24.4 2.1 %reshape.356 = bf16[16,20,1536]{2,1,0:T(8,128)(2,1)} reshape(bf16[320,1536]{1,0:T(8,128)(2,1)} %convolution_convert_fusion.1) | data formatting | bytes 1966080 | tf_op jit(solution)/shard_map/reshape | solution.py:381
  26.5 38.6 %all_to_all.10 = bf16[16,20,1536]{2,1,0:T(8,128)(2,1)} all-to-all(bf16[16,20,1536]{2,1,0:T(8,128)(2,1)} %reshape.356), channel_id=1, replica_groups=mesh['expert'=16,'fsdp'=2] {'expert'}, dimensions={0} | all-to-all | bytes 1966080 | tf_op jit(solution)/shard_map/all_to_all | solution.py:380
  65.2 2.1 %reshape.357 = bf16[320,1536]{1,0:T(8,128)(2,1)} reshape(bf16[16,20,1536]{2,1,0:T(8,128)(2,1)} %all_to_all.10) | data formatting | bytes 1966080 | tf_op jit(solution)/shard_map/reshape | solution.py:386
  67.3 1.4 constant_dynamic-update-slice_fusion.1
  68.7 1.4 collective-permute-done.3
  70.2 1.0 multiply_convert_fusion
  71.2 1.0 copy-done.74
  72.2 0.9 fusion.32
  73.2 1.4 fusion.18
  74.6 1.0 fusion.34
  75.6 1.1 fusion.22
  77.3 0.8 convert_bitcast_fusion.1
  78.1 0.7 copy.103
  78.8 1.3 collective-permute-done.4
  80.1 3.0 %fusion.21 = bf16[320,1536]{1,0:T(8,128)(2,1)} fusion(f32[640,768]{1,0:T(8,128)} %copy-done, f32[640,768]{1,0:T(8,128)} %copy-done.1, bf16[320,1536]{1,0:T(8,128)(2,1)} %collective-permute-done.4), kind=kLoop, calls=%fused_computation.37 | loop fusion | flops 1966080 | bytes 5898240 | tf_op jit(solution)/shard_map/convert_element_type | solution.py:404
  83.1 2.2 %reshape.358 = bf16[16,20,1536]{2,1,0:T(8,128)(2,1)} reshape(bf16[320,1536]{1,0:T(8,128)(2,1)} %fusion.21) | data formatting | bytes 1966080 | tf_op jit(solution)/shard_map/reshape | solution.py:406
  85.2 4.6 %all-to-all-start.1 = ((bf16[16,20,1536]{2,1,0:T(8,128)(2,1)}), bf16[16,20,1536]{2,1,0:T(8,128)(2,1)}, u32[]{:S(2)}, u32[]{:S(2)}) async-start(bf16[16,20,1536]{2,1,0:T(8,128)(2,1)} %reshape.358), calls=%async_computation.1 | async-start | bytes 2359296 | tf_op jit(solution)/shard_map/all_to_all | solution.py:405
  89.8 1.0 convert_bitcast_fusion
  90.8 0.9 copy.101
  91.7 9.1 %convert_subtract_fusion.1 = (f32[1,768,768]{2,1,0:T(8,128)}, f32[1,768,768]{2,1,0:T(8,128)}, f32[1,768,768]{2,1,0:T(8,128)}) fusion(bf16[1,768,768]{2,1,0:T(8,128)(2,1)} %param.33, f32[1,768,768]{2,1,0:T(8,128)} %param.35, f32[1,768,768]{2,1,0:T(8,128)} %param.34, bf16[640,768]{1,0:T(8,128)(2,1)} %copy-done.76, bf16[640,1536]{1,0:T(8,128)(2,1)} %copy-done.22), kind=kOutput, calls=%fused_computation.13 | convolution fusion | flops 764411904 | bytes 14942208 | tf_op jit(solution)/shard_map/rd,rh->dh/dot_general | solution.py:412
  100.9 5.7 %convert_subtract_fusion = (f32[1,768,768]{2,1,0:T(8,128)}, f32[1,768,768]{2,1,0:T(8,128)}, f32[1,768,768]{2,1,0:T(8,128)}) fusion(bf16[1,768,768]{2,1,0:T(8,128)(2,1)S(1)} %copy-done.75, f32[1,768,768]{2,1,0:T(8,128)S(1)} %copy-done.71, f32[1,768,768]{2,1,0:T(8,128)S(1)} %copy-done.72, bf16[640,768]{1,0:T(8,128)(2,1)S(1)} %copy-done.78, ...), kind=kOutput, calls=%fused_computation.11 | convolution fusion | flops 764411904 | bytes 14942208 | tf_op jit(solution)/shard_map/rh,rd->hd/dot_general | solution.py:413
  106.5 10.2 %all-to-all-done.1 = bf16[16,20,1536]{2,1,0:T(8,128)(2,1)} async-done(((bf16[16,20,1536]{2,1,0:T(8,128)(2,1)}), bf16[16,20,1536]{2,1,0:T(8,128)(2,1)}, u32[]{:S(2)}, u32[]{:S(2)}) %all-to-all-start.1) | async-done | bytes 983072 | tf_op jit(solution)/shard_map/all_to_all | solution.py:405
  116.7 2.1 %reshape.359 = bf16[320,1536]{1,0:T(8,128)(2,1)} reshape(bf16[16,20,1536]{2,1,0:T(8,128)(2,1)} %all-to-all-done.1) | data formatting | bytes 1966080 | tf_op jit(solution)/shard_map/reshape | solution.py:411
  119.0 1.6 fusion.92
  120.6 0.8 fusion.66
  121.4 1.1 multiply_reduce_fusion.1
  122.7 1.4 convolution_convert_fusion.4
  124.2 1.0 convolution_convert_fusion.5
  125.2 1.0 copy.87
  126.2 1.7 multiply_reduce_fusion
  127.9 1.4 fusion.85
  130.5 1.1 fusion.38
  131.6 1.7 copy.91
  133.4 0.8 fusion.49
  134.7 0.7 fusion.39
  135.4 0.7 reshape.364
  136.7 1.0 fusion.71
  138.7 1.1 convolution_convert_fusion
  139.8 2.8 %pad_maximum_fusion = bf16[768,3072]{1,0:T(8,128)(2,1)} fusion(bf16[768,768]{1,0:T(8,128)(2,1)S(1)} %convolution_convert_fusion.2, bf16[768,2304]{1,0:T(8,128)(2,1)S(1)} %convolution_convert_fusion), kind=kLoop, calls=%fused_computation.1 | loop fusion | flops 9437184 | bytes 9437184 | tf_op jit(solution)/shard_map/concatenate | solution.py:488
  142.7 11.6 %convert_element_type.181 = bf16[16,2,24,3,2,512]{5,4,3,2,1,0:T(2,128)(2,1)} reshape(bf16[768,3072]{1,0:T(8,128)(2,1)} %pad_maximum_fusion) | data formatting | bytes 9437184 | tf_op jit(solution)/shard_map/convert_element_type | solution.py:223
  154.3 3.7 %copy.90 = bf16[16,2,24,3,2,512]{5,2,4,0,3,1:T(8,128)(2,1)S(1)} copy(bf16[16,2,24,3,2,512]{5,4,3,2,1,0:T(2,128)(2,1)} %convert_element_type.181) | data formatting | bytes 9437184 | tf_op jit(solution)/shard_map/convert_element_type | solution.py:223
  158.0 0.7 fusion.23
  158.8 0.7 fusion.25
  159.8 39.6 %shard_map.416 = (f32[3,48,512]{2,1,0:T(8,128)S(1)}, f32[16,768]{1,0:T(8,128)S(1)}) custom-call(bf16[2,3,2,2,2,2,48,512]{7,6,5,4,3,2,1,0:T(8,128)(2,1)S(1)} %bitcast.104, f32[16,768]{1,0:T(8,128)S(1)} %pad.9.small), custom_call_target="tpu_custom_call" | custom-call | tf_op jit(solution)/shard_map/pallas_call | solution.py:233
  200.1 0.9 fusion.62
  201.6 0.6 convert_subtract_fusion.2
  202.3 0.6 convert_subtract_fusion.4
  202.9 0.6 convert_subtract_fusion.3
  203.5 2.3 %multiply_subtract_fusion = (f32[1,55296]{1,0:T(1,128)}, f32[1,55296]{1,0:T(1,128)}, f32[1,55296]{1,0:T(1,128)}) fusion(f32[1,55296]{1,0:T(1,128)S(1)} %bitcast.124, f32[1,55296]{1,0:T(1,128)S(1)} %bitcast.125, f32[1,55296]{1,0:T(1,128)S(1)} %copy-done.25, f32[1,55296]{1,0:T(1,128)S(1)} %copy-done.26), kind=kLoop, calls=%fused_computation.143 | loop fusion | flops 829440 | bytes 1548288 | tf_op jit(solution)/shard_map/sub | solution.py:62
  205.9 1.2 multiply_subtract_fusion.1
  (210 shorter events, 11.8 us)
Async XLA Ops:
  0.7 5.6 %collective-permute-start = (bf16[384,2304]{1,0:T(8,128)(2,1)}, bf16[384,2304]{1,0:T(8,128)(2,1)S(1)}, u32[]{:S(2)}, u32[]{:S(2)}) collective-permute-start(bf16[384,2304]{1,0:T(8,128)(2,1)} %param.27), channel_id=1, source_target_pairs={{0,1},{1,0},{2,3},{3,2},{4,5},{5,4},{6,7},{7,6},{8,9},{9,8},{10,11... | collective-permute-start | bytes 5308424 | tf_op jit(solution)/shard_map/ppermute | solution.py:67
  1.2 18.0 %collective-permute-start.2 = (bf16[384,768]{1,0:T(8,128)(2,1)}, bf16[384,768]{1,0:T(8,128)(2,1)}, u32[]{:S(2)}, u32[]{:S(2)}) collective-permute-start(bf16[384,768]{1,0:T(8,128)(2,1)} %param.30), channel_id=1, source_target_pairs={{0,1},{1,0},{2,3},{3,2},{4,5},{5,4},{6,7},{7,6},{8,9},{9,8},{10,11... | collective-permute-start | bytes 1769480 | tf_op jit(solution)/shard_map/ppermute | solution.py:67
  2.1 4.7 %copy-start.33 = (f32[768]{0:T(1024)}, f32[768]{0:T(1024)S(1)}, u32[]{:S(2)}) copy-start(f32[768]{0:T(1024)S(1)} %get-tuple-element.55) | copy-start | bytes 9220
  3.1 3.6 %copy-start.63 = (f32[128]{0:T(128)}, f32[128]{0:T(128)S(1)}, u32[]{:S(2)}) copy-start(f32[128]{0:T(128)S(1)} %add_rsqrt_fusion.1) | copy-start | bytes 1540
  4.2 2.6 %copy-start.13 = (bf16[128,768]{1,0:T(8,128)(2,1)}, bf16[128,768]{1,0:T(8,128)(2,1)S(1)}, u32[]{:S(2)}) copy-start(bf16[128,768]{1,0:T(8,128)(2,1)S(1)} %fusion.58) | copy-start | bytes 589828
  6.2 2.7 %copy-start.43 = (bf16[32,12]{0,1:T(8,128)(2,1)S(1)}, bf16[32,12]{0,1:T(8,128)(2,1)}, u32[]{:S(2)}) copy-start(bf16[32,12]{0,1:T(8,128)(2,1)} %param.45) | copy-start | bytes 2308
  7.7 5.1 %collective-permute-start.1 = (bf16[128,1536]{1,0:T(8,128)(2,1)}, bf16[128,1536]{1,0:T(8,128)(2,1)}, u32[]{:S(2)}, u32[]{:S(2)}) collective-permute-start(bf16[128,1536]{1,0:T(8,128)(2,1)} %slice.78), channel_id=1, source_target_pairs={{0,1},{1,0},{2,3},{3,2},{4,5},{5,4},{6,7},{7,6},{8,9},{9,8},{10,11... | collective-permute-start | bytes 1179656 | tf_op jit(solution)/shard_map/ppermute | solution.py:67
  9.7 2.2 %slice-start = ((bf16[128,2304]{1,0:T(8,128)(2,1)}), bf16[128,768]{1,0:T(8,128)(2,1)S(1)}, s32[]{:S(2)}) async-start(bf16[128,2304]{1,0:T(8,128)(2,1)} %copy-done.9), calls=%async_computation.2 | async-start | bytes 393216 | tf_op jit(solution)/shard_map/slice | solution.py:344
  11.3 3.6 %copy-start.3 = (f32[128,256,12]{1,0,2:T(8,128)S(1)}, f32[128,256,12]{1,0,2:T(8,128)}, u32[]{:S(2)}) copy-start(f32[128,256,12]{1,0,2:T(8,128)} %copy.86) | copy-start | bytes 4718596
  14.9 2.1 %copy-start.6 = (bf16[256,768]{0,1:T(8,128)(2,1)}, bf16[256,768]{0,1:T(8,128)(2,1)S(1)}, u32[]{:S(2)}) copy-start(bf16[256,768]{0,1:T(8,128)(2,1)S(1)} %copy.85) | copy-start | bytes 1179652
  16.5 2.3 %copy-start.4 = (bf16[384,768]{1,0:T(8,128)(2,1)S(1)}, bf16[384,768]{1,0:T(8,128)(2,1)}, u32[]{:S(2)}) copy-start(bf16[384,768]{1,0:T(8,128)(2,1)} %param.30) | copy-start | bytes 1769476
  17.1 2.1 %copy-start.5 = (bf16[128,768]{1,0:T(8,128)(2,1)S(1)}, bf16[128,768]{1,0:T(8,128)(2,1)}, u32[]{:S(2)}) copy-start(bf16[128,768]{1,0:T(8,128)(2,1)} %param.25) | copy-start | bytes 589828
  18.8 2.0 copy-start.27
  18.8 3.4 %copy-start.45 = (s32[128]{0:T(128)S(1)}, s32[128]{0:T(128)}, u32[]{:S(2)}) copy-start(s32[128]{0:T(128)} %param.48) | copy-start | bytes 1540
  18.8 4.0 %copy-start.16 = (bf16[128,768]{1,0:T(8,128)(2,1)S(1)}, bf16[128,768]{1,0:T(8,128)(2,1)}, u32[]{:S(2)}) copy-start(bf16[128,768]{1,0:T(8,128)(2,1)} %param.26) | copy-start | bytes 589828
  18.8 4.1 %copy-start.38 = (s32[320]{0:T(512)S(1)}, s32[320]{0:T(512)}, u32[]{:S(2)}) copy-start(s32[320]{0:T(512)} %get-tuple-element.92) | copy-start | bytes 3844
  18.9 4.1 %copy-start.40 = (s32[320]{0:T(512)S(1)}, s32[320]{0:T(512)}, u32[]{:S(2)}) copy-start(s32[320]{0:T(512)} %get-tuple-element.93) | copy-start | bytes 3844
  18.9 4.0 %copy-start.67 = (s32[128]{0:T(128)S(1)}, s32[128]{0:T(128)}, u32[]{:S(2)}) copy-start(s32[128]{0:T(128)} %param.49) | copy-start | bytes 1540
  67.3 2.9 %copy-start.73 = (bf16[1,768,768]{2,1,0:T(8,128)(2,1)S(1)}, bf16[1,768,768]{2,1,0:T(8,128)(2,1)}, u32[]{:S(2)}) copy-start(bf16[1,768,768]{2,1,0:T(8,128)(2,1)} %param.33) | copy-start | bytes 3538948
  67.3 2.8 %collective-permute-start.3 = (bf16[320,1536]{1,0:T(8,128)(2,1)}, bf16[320,1536]{1,0:T(8,128)(2,1)S(1)}, u32[]{:S(2)}, u32[]{:S(2)}) collective-permute-start(bf16[320,1536]{1,0:T(8,128)(2,1)} %reshape.357), channel_id=1, source_target_pairs={{0,1},{1,0},{2,3},{3,2},{4,5},{5,4},{6,7},{7,6},{8,9},{9,8},{10,11... | collective-permute-start | bytes 2949128 | tf_op jit(solution)/shard_map/ppermute | solution.py:67
  70.2 3.0 %copy-start.22 = (bf16[640,1536]{1,0:T(8,128)(2,1)}, bf16[640,1536]{1,0:T(8,128)(2,1)S(1)}, u32[]{:S(2)}) copy-start(bf16[640,1536]{1,0:T(8,128)(2,1)S(1)} %constant_dynamic-update-slice_fusion) | copy-start | bytes 5898244
  70.2 2.1 copy-start.74
  73.2 2.4 %copy-start = (f32[640,768]{1,0:T(8,128)}, f32[640,768]{1,0:T(8,128)S(1)}, u32[]{:S(2)}) copy-start(f32[640,768]{1,0:T(8,128)S(1)} %fusion.32) | copy-start | bytes 5898244
  77.2 2.9 %collective-permute-start.4 = (bf16[320,1536]{1,0:T(8,128)(2,1)}, bf16[320,1536]{1,0:T(8,128)(2,1)}, u32[]{:S(2)}, u32[]{:S(2)}) collective-permute-start(bf16[320,1536]{1,0:T(8,128)(2,1)} %fusion.22), channel_id=1, source_target_pairs={{0,1},{1,0},{2,3},{3,2},{4,5},{5,4},{6,7},{7,6},{8,9},{9,8},{10,11... | collective-permute-start | bytes 2949128 | tf_op jit(solution)/shard_map/ppermute | solution.py:67
  85.2 31.5 %all-to-all-start.1 = ((bf16[16,20,1536]{2,1,0:T(8,128)(2,1)}), bf16[16,20,1536]{2,1,0:T(8,128)(2,1)}, u32[]{:S(2)}, u32[]{:S(2)}) async-start(bf16[16,20,1536]{2,1,0:T(8,128)(2,1)} %reshape.358), calls=%async_computation.1 | async-start | bytes 2359296 | tf_op jit(solution)/shard_map/all_to_all | solution.py:405
  91.7 9.1 %copy-start.23 = (bf16[640,1536]{1,0:T(8,128)(2,1)S(1)}, bf16[640,1536]{1,0:T(8,128)(2,1)}, u32[]{:S(2)}) copy-start(bf16[640,1536]{1,0:T(8,128)(2,1)} %copy-done.22) | copy-start | bytes 5898244
  91.7 9.1 %copy-start.71 = (f32[1,768,768]{2,1,0:T(8,128)S(1)}, f32[1,768,768]{2,1,0:T(8,128)}, u32[]{:S(2)}) copy-start(f32[1,768,768]{2,1,0:T(8,128)} %param.38) | copy-start | bytes 7077892
  91.7 9.1 %copy-start.72 = (f32[1,768,768]{2,1,0:T(8,128)S(1)}, f32[1,768,768]{2,1,0:T(8,128)}, u32[]{:S(2)}) copy-start(f32[1,768,768]{2,1,0:T(8,128)} %param.37) | copy-start | bytes 7077892
  91.7 9.1 %copy-start.75 = (bf16[1,768,768]{2,1,0:T(8,128)(2,1)S(1)}, bf16[1,768,768]{2,1,0:T(8,128)(2,1)}, u32[]{:S(2)}) copy-start(bf16[1,768,768]{2,1,0:T(8,128)(2,1)} %param.36) | copy-start | bytes 3538948
  91.7 9.1 %copy-start.78 = (bf16[640,768]{1,0:T(8,128)(2,1)S(1)}, bf16[640,768]{1,0:T(8,128)(2,1)}, u32[]{:S(2)}) copy-start(bf16[640,768]{1,0:T(8,128)(2,1)} %copy-done.77) | copy-start | bytes 2949124
  106.5 12.4 %copy-start.39 = (s32[320]{0:T(512)S(1)}, s32[320]{0:T(512)}, u32[]{:S(2)}) copy-start(s32[320]{0:T(512)} %get-tuple-element.92) | copy-start | bytes 3844
  106.5 12.4 %copy-start.41 = (s32[320]{0:T(512)S(1)}, s32[320]{0:T(512)}, u32[]{:S(2)}) copy-start(s32[320]{0:T(512)} %get-tuple-element.93) | copy-start | bytes 3844
  106.5 12.4 %copy-start.46 = (s32[128]{0:T(128)S(1)}, s32[128]{0:T(128)}, u32[]{:S(2)}) copy-start(s32[128]{0:T(128)} %param.48) | copy-start | bytes 1540
  106.5 12.4 %copy-start.68 = (s32[128]{0:T(128)S(1)}, s32[128]{0:T(128)}, u32[]{:S(2)}) copy-start(s32[128]{0:T(128)} %param.49) | copy-start | bytes 1540
  106.5 14.1 %copy-start.66 = (f32[128]{0:T(128)S(1)}, f32[128]{0:T(128)}, u32[]{:S(2)}) copy-start(f32[128]{0:T(128)} %copy-done.65) | copy-start | bytes 1540
  118.9 2.5 %copy-start.28 = (bf16[768,8]{0,1:T(8,128)(2,1)S(1)}, bf16[768,8]{0,1:T(8,128)(2,1)}, u32[]{:S(2)}) copy-start(bf16[768,8]{0,1:T(8,128)(2,1)} %param.39) | copy-start | bytes 36868
  118.9 2.5 %copy-start.49 = (f32[128]{0:T(128)S(1)}, f32[128]{0:T(128)}, u32[]{:S(2)}) copy-start(f32[128]{0:T(128)} %copy-done.48) | copy-start | bytes 1540
  118.9 2.5 %copy-start.52 = (f32[128]{0:T(128)S(1)}, f32[128]{0:T(128)}, u32[]{:S(2)}) copy-start(f32[128]{0:T(128)} %copy-done.51) | copy-start | bytes 1540
  118.9 2.5 %copy-start.56 = (f32[128]{0:T(128)S(1)}, f32[128]{0:T(128)}, u32[]{:S(2)}) copy-start(f32[128]{0:T(128)} %copy-done.55) | copy-start | bytes 1540
  130.5 2.8 %copy-start.2 = (f32[12,64,256]{2,1,0:T(8,128)S(1)}, f32[12,64,256]{2,1,0:T(8,128)}, u32[]{:S(2)}) copy-start(f32[12,64,256]{2,1,0:T(8,128)} %fusion.85) | copy-start | bytes 2359300
  133.3 2.7 %copy-start.42 = (f32[768]{0:T(1024)S(1)}, f32[768]{0:T(1024)}, u32[]{:S(2)}) copy-start(f32[768]{0:T(1024)} %get-tuple-element.50) | copy-start | bytes 9220
  133.4 3.3 %copy-start.47 = (s32[128]{0:T(128)S(1)}, s32[128]{0:T(128)}, u32[]{:S(2)}) copy-start(s32[128]{0:T(128)} %param.48) | copy-start | bytes 1540
  133.4 3.3 %copy-start.50 = (f32[128]{0:T(128)S(1)}, f32[128]{0:T(128)}, u32[]{:S(2)}) copy-start(f32[128]{0:T(128)} %copy-done.48) | copy-start | bytes 1540
  133.4 3.3 %copy-start.53 = (f32[128]{0:T(128)S(1)}, f32[128]{0:T(128)}, u32[]{:S(2)}) copy-start(f32[128]{0:T(128)} %copy-done.51) | copy-start | bytes 1540
  133.4 3.3 %copy-start.57 = (f32[128]{0:T(128)S(1)}, f32[128]{0:T(128)}, u32[]{:S(2)}) copy-start(f32[128]{0:T(128)} %copy-done.55) | copy-start | bytes 1540
  133.4 3.3 %copy-start.70 = (f32[128]{0:T(128)S(1)}, f32[128]{0:T(128)}, u32[]{:S(2)}) copy-start(f32[128]{0:T(128)} %copy-done.69) | copy-start | bytes 1540
  134.2 3.9 %collective-permute-start.5 = (bf16[128,1536]{0,1:T(8,128)(2,1)}, bf16[128,1536]{0,1:T(8,128)(2,1)S(1)}, u32[]{:S(2)}, u32[]{:S(2)}) collective-permute-start(bf16[128,1536]{0,1:T(8,128)(2,1)} %fusion.49), channel_id=1, source_target_pairs={{0,1},{1,0},{2,3},{3,2},{4,5},{5,4},{6,7},{7,6},{8,9},{9,8},{10,11... | collective-permute-start | bytes 1179656 | tf_op jit(solution)/shard_map/ppermute | solution.py:67
  154.3 3.7 %copy-start.10 = (bf16[384,2304]{1,0:T(8,128)(2,1)S(1)}, bf16[384,2304]{1,0:T(8,128)(2,1)}, u32[]{:S(2)}) copy-start(bf16[384,2304]{1,0:T(8,128)(2,1)} %param.27) | copy-start | bytes 5308420
  154.3 3.7 %copy-start.12 = (bf16[384,2304]{1,0:T(8,128)(2,1)S(1)}, bf16[384,2304]{1,0:T(8,128)(2,1)}, u32[]{:S(2)}) copy-start(bf16[384,2304]{1,0:T(8,128)(2,1)} %copy-done.11) | copy-start | bytes 5308420
  199.4 2.2 %copy-start.29 = (bf16[768,8]{0,1:T(8,128)(2,1)S(1)}, bf16[768,8]{0,1:T(8,128)(2,1)}, u32[]{:S(2)}) copy-start(bf16[768,8]{0,1:T(8,128)(2,1)} %param.39) | copy-start | bytes 36868
  199.4 2.2 %copy-start.36 = (f32[768,8]{0,1:T(8,128)S(1)}, f32[768,8]{0,1:T(8,128)}, u32[]{:S(2)}) copy-start(f32[768,8]{0,1:T(8,128)} %param.41) | copy-start | bytes 73732
  199.4 2.2 %copy-start.37 = (f32[768,8]{0,1:T(8,128)S(1)}, f32[768,8]{0,1:T(8,128)}, u32[]{:S(2)}) copy-start(f32[768,8]{0,1:T(8,128)} %param.40) | copy-start | bytes 73732
  199.4 2.8 %copy-start.35 = (bf16[2,768]{1,0:T(2,128)(2,1)S(1)}, bf16[2,768]{1,0:T(2,128)(2,1)}, u32[]{:S(2)}) copy-start(bf16[2,768]{1,0:T(2,128)(2,1)} %param.42) | copy-start | bytes 9220
  199.4 2.8 %copy-start.60 = (f32[2,768]{1,0:T(2,128)S(1)}, f32[2,768]{1,0:T(2,128)}, u32[]{:S(2)}) copy-start(f32[2,768]{1,0:T(2,128)} %param.44) | copy-start | bytes 18436
  199.5 2.8 %copy-start.61 = (f32[2,768]{1,0:T(2,128)S(1)}, f32[2,768]{1,0:T(2,128)}, u32[]{:S(2)}) copy-start(f32[2,768]{1,0:T(2,128)} %param.43) | copy-start | bytes 18436
  199.5 3.4 %copy-start.44 = (bf16[32,12]{0,1:T(8,128)(2,1)S(1)}, bf16[32,12]{0,1:T(8,128)(2,1)}, u32[]{:S(2)}) copy-start(bf16[32,12]{0,1:T(8,128)(2,1)} %param.45) | copy-start | bytes 2308
  199.5 3.4 %copy-start.58 = (f32[32,12]{0,1:T(8,128)S(1)}, f32[32,12]{0,1:T(8,128)}, u32[]{:S(2)}) copy-start(f32[32,12]{0,1:T(8,128)} %param.47) | copy-start | bytes 4612
  199.5 3.4 %copy-start.59 = (f32[32,12]{0,1:T(8,128)S(1)}, f32[32,12]{0,1:T(8,128)}, u32[]{:S(2)}) copy-start(f32[32,12]{0,1:T(8,128)} %param.46) | copy-start | bytes 4612
  199.5 4.0 %copy-start.18 = (f32[1,1,24,2304]{3,1,2,0:T(1,128)S(1)}, f32[1,1,24,2304]{3,1,2,0:T(1,128)}, u32[]{:S(2)}) copy-start(f32[1,1,24,2304]{3,1,2,0:T(1,128)} %copy.101) | copy-start | bytes 663556
  199.5 4.0 %copy-start.25 = (f32[1,55296]{1,0:T(1,128)S(1)}, f32[1,55296]{1,0:T(1,128)}, u32[]{:S(2)}) copy-start(f32[1,55296]{1,0:T(1,128)} %param.29) | copy-start | bytes 663556
  199.5 4.0 %copy-start.26 = (f32[1,55296]{1,0:T(1,128)S(1)}, f32[1,55296]{1,0:T(1,128)}, u32[]{:S(2)}) copy-start(f32[1,55296]{1,0:T(1,128)} %param.28) | copy-start | bytes 663556
  200.1 5.8 %copy-start.24 = (f32[1,1,24,768]{3,1,2,0:T(1,128)S(1)}, f32[1,1,24,768]{3,1,2,0:T(1,128)}, u32[]{:S(2)}) copy-start(f32[1,1,24,768]{3,1,2,0:T(1,128)} %copy.103) | copy-start | bytes 221188
  200.1 5.8 %copy-start.31 = (f32[1,18432]{1,0:T(1,128)S(1)}, f32[1,18432]{1,0:T(1,128)}, u32[]{:S(2)}) copy-start(f32[1,18432]{1,0:T(1,128)} %param.32) | copy-start | bytes 221188
  200.1 5.8 %copy-start.32 = (f32[1,18432]{1,0:T(1,128)S(1)}, f32[1,18432]{1,0:T(1,128)}, u32[]{:S(2)}) copy-start(f32[1,18432]{1,0:T(1,128)} %param.31) | copy-start | bytes 221188
  (23 other events, 23.6 us)

commit v3 on v2

--- a/solution.py
+++ b/solution.py
@@ -1,4 +1,3 @@
-import functools
 import itertools
 
 import jax
@@ -103,7 +102,8 @@
     return value
 
 
-def owner_sum_kernel(bits, orders, grad, small, total, small_total, held, *rest):
+def owner_sum_kernel(bits, orders, lefts, rights, small, total, small_total, grad, held, *rest):
+    left_count = len(lefts)
     landed, (small_held, small_landed, send_sem, recv_sem, small_send, small_recv) = (
         rest[: bits + 1],
         rest[bits + 1 :],
@@ -187,9 +187,50 @@
             else:
                 held[(piece, *held_at)] = (before + arrived).astype(held.dtype)
 
+    edges = [0]
+    for right in rights:
+        edges.append(edges[-1] + right.shape[1])
+    width = grad.shape[-1]
+    block = grad.shape[-2] // 2
+    chunk = min(4, 1 << bits)
+
+    def product(first_row, row_count, first_column):
+        parts = []
+        for index in range(left_count):
+            begin = max(first_column, edges[index])
+            end = min(first_column + width, edges[index + 1])
+            if begin < end:
+                parts.append(
+                    jnp.dot(
+                        lefts[index][first_row : first_row + row_count, :],
+                        rights[index][:, begin - edges[index] : end - edges[index]],
+                        preferred_element_type=jnp.float32,
+                    )
+                )
+        return parts[0] if len(parts) == 1 else jnp.concatenate(parts, axis=1)
+
+    def make_piece(piece):
+        for first in range(0, 1 << bits, chunk):
+            sides = [
+                product(
+                    first * 2 * block, chunk * 2 * block, (2 * piece + side) * width
+                )
+                for side in range(2)
+            ]
+            for offset in range(chunk):
+                chip = first + offset
+                chip_at = tuple((chip >> bit) & 1 for bit in range(bits - 1, -1, -1))
+                for to_core in range(2):
+                    row = (2 * offset + to_core) * block
+                    joined = jnp.concatenate(
+                        [side[row : row + block] for side in sides], axis=0
+                    )
+                    grad[(to_core, piece, *chip_at)] = joined.astype(grad.dtype)
+
+    small_copy(0).start()
     for piece in range(pieces):
+        make_piece(piece)
         piece_copy(piece, 0).start()
-    small_copy(0).start()
     for step in range(bits + 1):
         for piece in range(pieces):
             piece_copy(piece, step).wait_recv()
@@ -210,33 +251,35 @@
         small_copy(step).wait_send()
 
 
-def owner_sum(grad, small):
+def owner_sum(lefts, rights, small):
     n_expert = lax.axis_size("expert")
     bits = n_expert.bit_length() - 1
-    rows, columns = grad.shape
+    rows = lefts[0].shape[0]
+    columns = sum(right.shape[1] for right in rights)
     block = rows // (2 * n_expert)
     pieces = 3
     width = columns // (2 * pieces)
     order = list(range(bits))
     orders = [order[shift:] + order[:shift] for shift in range(pieces)]
-    spread = (
-        grad.astype(jnp.bfloat16)
-        .reshape(n_expert, 2, block, pieces, 2, width)
-        .transpose(1, 3, 0, 4, 2, 5)
-        .reshape((2, pieces) + (2,) * bits + (2 * block, width))
-    )
     vmem = pl.BlockSpec(memory_space=pltpu.VMEM)
+    count = len(lefts)
+
+    def kernel(*refs):
+        owner_sum_kernel(bits, orders, refs[:count], refs[count : 2 * count], *refs[2 * count :])
+
     slots = [
+        pltpu.VMEM((2, pieces) + (2,) * bits + (2 * block, width), jnp.bfloat16)
+    ] + [
         pltpu.VMEM((pieces,) + (2,) * (bits - step) + (2 * block, width), jnp.bfloat16)
         for step in [0] + list(range(bits + 1))
     ]
     total, small_total = pl.pallas_call(
-        functools.partial(owner_sum_kernel, bits, orders),
+        kernel,
         out_shape=(
             jax.ShapeDtypeStruct((pieces, 2 * block, width), jnp.float32),
             jax.ShapeDtypeStruct(small.shape, jnp.float32),
         ),
-        in_specs=[vmem, vmem],
+        in_specs=[vmem] * (2 * count + 1),
         out_specs=(vmem, vmem),
         scratch_shapes=slots
         + [
@@ -250,7 +293,7 @@
         compiler_params=pltpu.CompilerParams(
             collective_id=0, has_side_effects=True, vmem_limit_bytes=32 * 2**20
         ),
-    )(spread, small)
+    )(*lefts, *rights, small)
     total = total.reshape(pieces, 2, block, width).transpose(2, 0, 1, 3).reshape(block, columns)
     return total, small_total
 
@@ -485,7 +528,7 @@
     if block % 8 == 0:
         small = jnp.pad(small, ((0, -small.shape[0] % 8), (0, 0)))
         weight_sum, small = owner_sum(
-            jnp.concatenate([weight_grad(qkv_grad), out_weight_grad], axis=1), small
+            (normed_low.T, context.T), (qkv_grad, attention_grad), small
         )
         qkv_sum = weight_sum[:, : 3 * model_width].reshape(1, -1)
         out_sum = weight_sum[:, 3 * model_width :].reshape(1, -1)

time: 208 us -> 183 us (0.88)
  local copies, waits for them, and re-layouts: 42.2 us -> 20.1 us
  other arithmetic: 24.1 us -> 21 us
    convert_element_type x2 -> x0, local copies, waits for them, and re-layouts: 15.3 us -> none  [owner_sum(): grad.astype(jnp.bfloat16).reshape(n_expert, 2, block, pieces, 2, width)]
    concatenate x1, other arithmetic: 2.82 us -> 0.04 us  [local(): qkv_grad = jnp.concatenate([query_grad, key_value_own], axis=1)]
    unnamed x165 -> x167, local copies, waits for them, and re-layouts: 8.77 us -> 8.2 us
  transfers between devices with their start and end apart: 7 -> 7, of which waited for: 3 -> 2; matrix products, arithmetic and copies ran while one was open for 19% -> 19% of each run, Pallas kernels for 0% -> 0%
where the time goes in v3:
time: 183 us; the launch traced here: 182 us
  Pallas kernels  41.1 us (22%)
  matrix products  40.2 us (22%)
  blocking collectives  38.4 us (21%)
  other arithmetic  21 us (11%)
  local copies, waits for them, and re-layouts  20.1 us (11%)
  waiting for transfers between devices  13.3 us (7%)
  starting transfers between devices  5.94 us (3%)
  between operations  2.08 us (1%)
    pallas_call x1, Pallas kernels, owner_sum(): pl.pallas_call(kernel, out_shape=(jax.ShapeDtypeStruct((pieces, 2 * block...  41.1 us
    all_to_all x1, blocking collectives, local(): lax.all_to_all(dispatched.reshape(n_expert, capacity, 2 * model_width), '...  38.4 us
    all_to_all x1, waiting for transfers between devices, local(): lax.all_to_all(summed.reshape(n_expert, capacity, 2 * model_width), 'expe...  10.9 us
    dot_general x1, matrix products, local(): jnp.einsum('rd,rh->dh', expert_in, pre_grad, preferred_element_type=jnp.f...  8.82 us
    unnamed x167, local copies, waits for them, and re-layouts  8.2 us
    dot_general x1, matrix products, local(): jnp.einsum('rh,rd->hd', activated, grad_in, preferred_element_type=jnp.fl...  5.65 us
    sub x5, other arithmetic, adam_step(): weight - rate * (moment_hat / (jnp.sqrt(square_hat) + ADAM_EPS) + decay *...  5.44 us
    all_to_all x1, starting transfers between devices, local(): lax.all_to_all(summed.reshape(n_expert, capacity, 2 * model_width), 'expe...  4.7 us
  transfers between devices with their start and end apart: 7, of which 2 were waited for; matrix products, arithmetic and copies ran while one was open for 19% of the time, Pallas kernels for 0%

profile of v3, /device:TPU:0, one launch (start us, length us, event | category | flops | bytes accessed | tf_op | source)
XLA Modules:
  0.0 182.1 jit_solution(1909705085510749319)
XLA Ops:
  0.7 0.5 collective-permute-start
  1.3 0.8 convert_reduce_fusion
  2.1 1.0 fusion.64
  3.1 1.0 fusion.58
  4.2 1.9 %fusion.103 = f32[128,2304]{1,0:T(8,128)S(1)} fusion(bf16[384,2304]{1,0:T(8,128)(2,1)} %param.27, bf16[128,768]{1,0:T(8,128)(2,1)S(1)} %fusion.58, s32[]{:T(128)S(6)} %select_n.101), kind=kOutput, calls=%fused_computation.161 | convolution fusion | flops 226492416 | bytes 3047428 | tf_op jit(solution)/shard_map/dot_general | solution.py:357
  6.2 0.5 fusion.2
  6.7 0.7 copy-done.14
  7.4 0.4 collective-permute-start.1
  8.1 0.7 fusion.1
  8.8 1.6 copy.90
  10.7 1.1 pad_maximum_fusion.3
  12.0 2.0 %fusion.151 = (f32[12,128]{1,0:T(8,128)S(1)}, f32[12,128,256]{2,1,0:T(8,128)S(1)}) fusion(f32[128,256,12]{1,0,2:T(8,128)} %copy.90, bf16[128,12,64]{0,2,1:T(8,128)(2,1)S(1)} %bitcast.115, bf16[256,12,64]{0,2,1:T(8,128)(2,1)S(1)} %bitcast.109), kind=kOutput, calls=%fused_computation.241 | convolution fusion | flops 51509760 | bytes 3741696 | tf_op jit(solution)/shard_map/qhd,khd->hqk/dot_general | solution.py:389
  14.1 0.5 exponential_reduce_fusion
  14.8 0.5 convolution_convert_fusion.1
  15.7 1.5 multiply_reduce_fusion.3
  18.3 1.5 convolution_convert_fusion
  19.8 1.3 reshape.350
  21.1 38.4 %all_to_all.10 = bf16[16,20,1536]{2,1,0:T(8,128)(2,1)} all-to-all(bf16[16,20,1536]{2,1,0:T(8,128)(2,1)S(1)} %reshape.350), channel_id=1, replica_groups=mesh['expert'=16,'fsdp'=2] {'expert'}, dimensions={0} | all-to-all | bytes 1966080 | tf_op jit(solution)/shard_map/all_to_all | solution.py:423
  59.5 1.4 reshape.351
  61.1 2.5 %collective-permute-done.3 = bf16[320,1536]{1,0:T(8,128)(2,1)S(1)} collective-permute-done((bf16[320,1536]{1,0:T(8,128)(2,1)S(1)}, bf16[320,1536]{1,0:T(8,128)(2,1)S(1)}, u32[]{:S(2)}, u32[]{:S(2)}) %collective-permute-start.3) | collective-permute-done | bytes 983072 | tf_op jit(solution)/shard_map/ppermute | solution.py:66
  63.6 1.0 multiply_convert_fusion
  64.7 1.0 copy-done.74
  65.7 0.9 fusion.32
  66.7 1.4 fusion.18
  68.1 1.0 fusion.34
  69.2 1.1 copy-done.1
  70.5 0.8 fusion.175
  71.3 1.1 copy.98.refs_0_
  72.4 0.8 convert_bitcast_fusion.1
  73.2 0.7 copy.108
  73.9 2.0 %fusion.21 = bf16[320,1536]{1,0:T(8,128)(2,1)S(1)} fusion(f32[640,768]{1,0:T(8,128)} %copy-done, f32[640,768]{1,0:T(8,128)} %copy-done.1, bf16[320,1536]{1,0:T(8,128)(2,1)} %collective-permute-done.4), kind=kLoop, calls=%fused_computation.35 | loop fusion | flops 1966080 | bytes 5898240 | tf_op jit(solution)/shard_map/convert_element_type | solution.py:447
  75.9 1.1 reshape.352
  77.1 4.7 %all-to-all-start.1 = ((bf16[16,20,1536]{2,1,0:T(8,128)(2,1)}), bf16[16,20,1536]{2,1,0:T(8,128)(2,1)}, u32[]{:S(2)}, u32[]{:S(2)}) async-start(bf16[16,20,1536]{2,1,0:T(8,128)(2,1)} %reshape.352), calls=%async_computation.1 | async-start | bytes 2359296 | tf_op jit(solution)/shard_map/all_to_all | solution.py:448
  81.8 1.0 convert_bitcast_fusion
  82.8 0.9 copy.106
  83.7 8.8 %convert_subtract_fusion.1 = (f32[1,768,768]{2,1,0:T(8,128)}, f32[1,768,768]{2,1,0:T(8,128)}, f32[1,768,768]{2,1,0:T(8,128)}) fusion(bf16[1,768,768]{2,1,0:T(8,128)(2,1)} %param.33, f32[1,768,768]{2,1,0:T(8,128)} %param.35, f32[1,768,768]{2,1,0:T(8,128)} %param.34, bf16[640,768]{1,0:T(8,128)(2,1)S(1)} %copy-done.77, bf16[640,1536]{1,0:T(8,128)(2,1)} %copy-done.24), kind=kOutput, calls=%fused_computation.11 | convolution fusion | flops 764411904 | bytes 14942208 | tf_op jit(solution)/shard_map/rd,rh->dh/dot_general | solution.py:455
  92.6 5.7 %convert_subtract_fusion = (f32[1,768,768]{2,1,0:T(8,128)}, f32[1,768,768]{2,1,0:T(8,128)}, f32[1,768,768]{2,1,0:T(8,128)}) fusion(bf16[1,768,768]{2,1,0:T(8,128)(2,1)S(1)} %copy-done.75, f32[1,768,768]{2,1,0:T(8,128)S(1)} %copy-done.71, f32[1,768,768]{2,1,0:T(8,128)S(1)} %copy-done.72, bf16[640,768]{1,0:T(8,128)(2,1)S(1)} %copy-done.79, ...), kind=kOutput, calls=%fused_computation.9 | convolution fusion | flops 764411904 | bytes 14942208 | tf_op jit(solution)/shard_map/rh,rd->hd/dot_general | solution.py:456
  98.2 10.9 %all-to-all-done.1 = bf16[16,20,1536]{2,1,0:T(8,128)(2,1)} async-done(((bf16[16,20,1536]{2,1,0:T(8,128)(2,1)}), bf16[16,20,1536]{2,1,0:T(8,128)(2,1)}, u32[]{:S(2)}, u32[]{:S(2)}) %all-to-all-start.1) | async-done | bytes 983072 | tf_op jit(solution)/shard_map/all_to_all | solution.py:448
  109.1 1.4 reshape.353
  110.5 1.2 fusion.92
  111.7 1.8 fusion.66
  113.6 1.1 multiply_reduce_fusion.1
  114.6 0.7 copy-done.7
  115.6 1.5 convolution_convert_fusion.2
  117.2 1.4 convolution_convert_fusion.3
  118.7 0.7 multiply_reduce_fusion
  119.5 1.4 fusion.85
  120.8 0.5 multiply_convert_fusion.1
  121.3 0.4 copy-done.17
  122.0 1.1 fusion.38
  123.1 1.7 copy.96
  125.1 0.9 copy-done.9
  126.4 0.8 fusion.49
  127.3 1.9 %fusion.39 = f32[32,12]{1,0:T(8,128)S(1)} fusion(bf16[12,128,256]{1,0,2:T(8,128)(2,1)} %copy.96, s32[128,256]{0,1:T(8,128)S(1)} %copy-done.23), kind=kOutput, calls=%fused_computation.70 | convolution fusion | flops 26214400 | bytes 919040 | tf_op jit(solution)/shard_map/evf,uvf->eu/dot_general | solution.py:504
  129.9 1.3 fusion.48
  131.6 0.7 fusion.23
  132.2 0.7 fusion.25
  133.2 41.1 %shard_map.416 = (f32[3,48,512]{2,1,0:T(8,128)S(1)}, f32[16,768]{1,0:T(8,128)S(1)}) custom-call(bf16[768,128]{1,0:T(8,128)(2,1)S(1)} %copy.98.refs_0_, bf16[768,128]{1,0:T(8,128)(2,1)S(1)} %bitcast.107, bf16[128,2304]{1,0:T(8,128)(2,1)S(1)} %pad_maximum_fusion.2.refs_2_, bf16[128,768]{1,0:T(8,128)(2,1)S(1)} %fusion.142.refs_3_, f32[16,768]{1,0:T(8,128)S(1)} %pad.9.refs_4_), custom_call_target="tpu_custom_call" | custom-call | tf_op jit(solution)/shard_map/pallas_call | solution.py:276
  175.1 1.0 fusion.62
  176.6 0.6 convert_subtract_fusion.2
  177.3 0.6 convert_subtract_fusion.4
  177.9 0.6 convert_subtract_fusion.3
  178.6 2.4 %multiply_subtract_fusion = (f32[1,55296]{1,0:T(1,128)}, f32[1,55296]{1,0:T(1,128)}, f32[1,55296]{1,0:T(1,128)}) fusion(f32[1,55296]{1,0:T(1,128)S(1)} %bitcast.122, f32[1,55296]{1,0:T(1,128)S(1)} %bitcast.123, f32[1,55296]{1,0:T(1,128)S(1)} %copy-done.27, f32[1,55296]{1,0:T(1,128)S(1)} %copy-done.28), kind=kLoop, calls=%fused_computation.140 | loop fusion | flops 829440 | bytes 1548288 | tf_op jit(solution)/shard_map/sub | solution.py:61
  180.9 1.2 multiply_subtract_fusion.1
  (212 shorter events, 6.7 us)
Async XLA Ops:
  0.7 5.5 %collective-permute-start = (bf16[384,2304]{1,0:T(8,128)(2,1)}, bf16[384,2304]{1,0:T(8,128)(2,1)S(1)}, u32[]{:S(2)}, u32[]{:S(2)}) collective-permute-start(bf16[384,2304]{1,0:T(8,128)(2,1)} %param.27), channel_id=1, source_target_pairs={{0,1},{1,0},{2,3},{3,2},{4,5},{5,4},{6,7},{7,6},{8,9},{9,8},{10,11... | collective-permute-start | bytes 5308424 | tf_op jit(solution)/shard_map/ppermute | solution.py:66
  1.2 14.5 %collective-permute-start.2 = (bf16[384,768]{1,0:T(8,128)(2,1)}, bf16[384,768]{1,0:T(8,128)(2,1)}, u32[]{:S(2)}, u32[]{:S(2)}) collective-permute-start(bf16[384,768]{1,0:T(8,128)(2,1)} %param.30), channel_id=1, source_target_pairs={{0,1},{1,0},{2,3},{3,2},{4,5},{5,4},{6,7},{7,6},{8,9},{9,8},{10,11... | collective-permute-start | bytes 1769480 | tf_op jit(solution)/shard_map/ppermute | solution.py:66
  3.1 3.0 %copy-start.54 = (f32[128]{0:T(128)}, f32[128]{0:T(128)S(1)}, u32[]{:S(2)}) copy-start(f32[128]{0:T(128)S(1)} %add_rsqrt_fusion.1) | copy-start | bytes 1540
  7.4 3.3 %collective-permute-start.1 = (bf16[128,1536]{1,0:T(8,128)(2,1)S(1)}, bf16[128,1536]{1,0:T(8,128)(2,1)}, u32[]{:S(2)}, u32[]{:S(2)}) collective-permute-start(bf16[128,1536]{1,0:T(8,128)(2,1)S(1)} %slice.78), channel_id=1, source_target_pairs={{0,1},{1,0},{2,3},{3,2},{4,5},{5,4},{6,7},{7,6},{8,9},{9,8},{10,11... | collective-permute-start | bytes 1179656 | tf_op jit(solution)/shard_map/ppermute | solution.py:66
  8.1 2.4 %copy-start.22 = (s32[128,256]{0,1:T(8,128)}, s32[128,256]{0,1:T(8,128)S(1)}, u32[]{:S(2)}) copy-start(s32[128,256]{0,1:T(8,128)S(1)} %fusion.93) | copy-start | bytes 393220
  10.4 7.5 %copy-start.40 = (s32[320]{0:T(512)}, s32[320]{0:T(512)S(1)}, u32[]{:S(2)}) copy-start(s32[320]{0:T(512)S(1)} %get-tuple-element.92) | copy-start | bytes 3844
  10.5 7.5 %copy-start.41 = (s32[320]{0:T(512)}, s32[320]{0:T(512)S(1)}, u32[]{:S(2)}) copy-start(s32[320]{0:T(512)S(1)} %get-tuple-element.93) | copy-start | bytes 3844
  10.7 3.4 %copy-start.16 = (bf16[128,768]{0,1:T(8,128)(2,1)}, bf16[128,768]{0,1:T(8,128)(2,1)S(1)}, u32[]{:S(2)}) copy-start(bf16[128,768]{0,1:T(8,128)(2,1)S(1)} %copy.88) | copy-start | bytes 589828
  12.0 2.6 %copy-start.3 = (bf16[256,768]{0,1:T(8,128)(2,1)}, bf16[256,768]{0,1:T(8,128)(2,1)S(1)}, u32[]{:S(2)}) copy-start(bf16[256,768]{0,1:T(8,128)(2,1)S(1)} %copy.89) | copy-start | bytes 1179652
  15.3 2.0 %copy-start.29 = (bf16[768,8]{0,1:T(8,128)(2,1)S(1)}, bf16[768,8]{0,1:T(8,128)(2,1)}, u32[]{:S(2)}) copy-start(bf16[768,8]{0,1:T(8,128)(2,1)} %param.39) | copy-start | bytes 36868
  15.3 2.4 %copy-start.48 = (s32[128]{0:T(128)S(1)}, s32[128]{0:T(128)}, u32[]{:S(2)}) copy-start(s32[128]{0:T(128)} %param.48) | copy-start | bytes 1540
  15.3 2.5 %copy-start.10 = (bf16[128,768]{1,0:T(8,128)(2,1)S(1)}, bf16[128,768]{1,0:T(8,128)(2,1)}, u32[]{:S(2)}) copy-start(bf16[128,768]{1,0:T(8,128)(2,1)} %param.26) | copy-start | bytes 589828
  15.4 3.0 %copy-start.66 = (s32[128]{0:T(128)S(1)}, s32[128]{0:T(128)}, u32[]{:S(2)}) copy-start(s32[128]{0:T(128)} %param.49) | copy-start | bytes 1540
  60.9 2.7 %copy-start.73 = (bf16[1,768,768]{2,1,0:T(8,128)(2,1)S(1)}, bf16[1,768,768]{2,1,0:T(8,128)(2,1)}, u32[]{:S(2)}) copy-start(bf16[1,768,768]{2,1,0:T(8,128)(2,1)} %param.33) | copy-start | bytes 3538948
  60.9 2.6 %collective-permute-start.3 = (bf16[320,1536]{1,0:T(8,128)(2,1)S(1)}, bf16[320,1536]{1,0:T(8,128)(2,1)S(1)}, u32[]{:S(2)}, u32[]{:S(2)}) collective-permute-start(bf16[320,1536]{1,0:T(8,128)(2,1)S(1)} %reshape.351), channel_id=1, source_target_pairs={{0,1},{1,0},{2,3},{3,2},{4,5},{5,4},{6,7},{7,6},{8,9},{9,8},{10,11... | collective-permute-start | bytes 2949128 | tf_op jit(solution)/shard_map/ppermute | solution.py:66
  63.6 3.0 %copy-start.24 = (bf16[640,1536]{1,0:T(8,128)(2,1)}, bf16[640,1536]{1,0:T(8,128)(2,1)S(1)}, u32[]{:S(2)}) copy-start(bf16[640,1536]{1,0:T(8,128)(2,1)S(1)} %constant_dynamic-update-slice_fusion) | copy-start | bytes 5898244
  63.6 2.1 %copy-start.74 = (bf16[1,768,768]{2,1,0:T(8,128)(2,1)S(1)}, bf16[1,768,768]{2,1,0:T(8,128)(2,1)}, u32[]{:S(2)}) copy-start(bf16[1,768,768]{2,1,0:T(8,128)(2,1)} %param.36) | copy-start | bytes 3538948
  64.7 2.0 %copy-start.78 = (bf16[640,768]{1,0:T(8,128)(2,1)}, bf16[640,768]{1,0:T(8,128)(2,1)S(1)}, u32[]{:S(2)}) copy-start(bf16[640,768]{1,0:T(8,128)(2,1)S(1)} %get-tuple-element.87) | copy-start | bytes 2949124
  66.6 2.4 %copy-start = (f32[640,768]{1,0:T(8,128)}, f32[640,768]{1,0:T(8,128)S(1)}, u32[]{:S(2)}) copy-start(f32[640,768]{1,0:T(8,128)S(1)} %fusion.32) | copy-start | bytes 5898244
  70.4 3.5 %collective-permute-start.4 = (bf16[320,1536]{1,0:T(8,128)(2,1)S(1)}, bf16[320,1536]{1,0:T(8,128)(2,1)}, u32[]{:S(2)}, u32[]{:S(2)}) collective-permute-start(bf16[320,1536]{1,0:T(8,128)(2,1)S(1)} %fusion.22), channel_id=1, source_target_pairs={{0,1},{1,0},{2,3},{3,2},{4,5},{5,4},{6,7},{7,6},{8,9},{9,8},{10,11... | collective-permute-start | bytes 2949128 | tf_op jit(solution)/shard_map/ppermute | solution.py:66
  77.1 6.6 %copy-start.77 = (bf16[640,768]{1,0:T(8,128)(2,1)S(1)}, bf16[640,768]{1,0:T(8,128)(2,1)}, u32[]{:S(2)}) copy-start(bf16[640,768]{1,0:T(8,128)(2,1)} %copy-done.76) | copy-start | bytes 2949124
  77.1 32.0 %all-to-all-start.1 = ((bf16[16,20,1536]{2,1,0:T(8,128)(2,1)}), bf16[16,20,1536]{2,1,0:T(8,128)(2,1)}, u32[]{:S(2)}, u32[]{:S(2)}) async-start(bf16[16,20,1536]{2,1,0:T(8,128)(2,1)} %reshape.352), calls=%async_computation.1 | async-start | bytes 2359296 | tf_op jit(solution)/shard_map/all_to_all | solution.py:448
  83.7 8.9 %copy-start.25 = (bf16[640,1536]{1,0:T(8,128)(2,1)S(1)}, bf16[640,1536]{1,0:T(8,128)(2,1)}, u32[]{:S(2)}) copy-start(bf16[640,1536]{1,0:T(8,128)(2,1)} %copy-done.24) | copy-start | bytes 5898244
  83.7 8.9 %copy-start.71 = (f32[1,768,768]{2,1,0:T(8,128)S(1)}, f32[1,768,768]{2,1,0:T(8,128)}, u32[]{:S(2)}) copy-start(f32[1,768,768]{2,1,0:T(8,128)} %param.38) | copy-start | bytes 7077892
  83.7 8.9 %copy-start.72 = (f32[1,768,768]{2,1,0:T(8,128)S(1)}, f32[1,768,768]{2,1,0:T(8,128)}, u32[]{:S(2)}) copy-start(f32[1,768,768]{2,1,0:T(8,128)} %param.37) | copy-start | bytes 7077892
  83.7 8.9 %copy-start.75 = (bf16[1,768,768]{2,1,0:T(8,128)(2,1)S(1)}, bf16[1,768,768]{2,1,0:T(8,128)(2,1)}, u32[]{:S(2)}) copy-start(bf16[1,768,768]{2,1,0:T(8,128)(2,1)} %param.36) | copy-start | bytes 3538948
  83.7 8.9 %copy-start.79 = (bf16[640,768]{1,0:T(8,128)(2,1)S(1)}, bf16[640,768]{1,0:T(8,128)(2,1)}, u32[]{:S(2)}) copy-start(bf16[640,768]{1,0:T(8,128)(2,1)} %copy-done.78) | copy-start | bytes 2949124
  110.4 3.1 %copy-start.65 = (f32[128]{0:T(128)S(1)}, f32[128]{0:T(128)}, u32[]{:S(2)}) copy-start(f32[128]{0:T(128)} %copy-done.64) | copy-start | bytes 1540
  110.4 3.1 %copy-start.30 = (bf16[768,8]{0,1:T(8,128)(2,1)S(1)}, bf16[768,8]{0,1:T(8,128)(2,1)}, u32[]{:S(2)}) copy-start(bf16[768,8]{0,1:T(8,128)(2,1)} %param.39) | copy-start | bytes 36868
  110.5 3.1 %copy-start.33 = (f32[128,8]{0,1:T(8,128)S(1)}, f32[128,8]{0,1:T(8,128)}, u32[]{:S(2)}) copy-start(f32[128,8]{0,1:T(8,128)} %copy-done.32) | copy-start | bytes 12292
  110.5 3.1 %copy-start.43 = (f32[128]{0:T(128)S(1)}, f32[128]{0:T(128)}, u32[]{:S(2)}) copy-start(f32[128]{0:T(128)} %copy-done.42) | copy-start | bytes 1540
  110.5 3.1 %copy-start.49 = (s32[128]{0:T(128)S(1)}, s32[128]{0:T(128)}, u32[]{:S(2)}) copy-start(s32[128]{0:T(128)} %param.48) | copy-start | bytes 1540
  110.5 3.1 %copy-start.52 = (f32[128]{0:T(128)S(1)}, f32[128]{0:T(128)}, u32[]{:S(2)}) copy-start(f32[128]{0:T(128)} %copy-done.51) | copy-start | bytes 1540
  110.5 3.1 %copy-start.58 = (f32[128]{0:T(128)S(1)}, f32[128]{0:T(128)}, u32[]{:S(2)}) copy-start(f32[128]{0:T(128)} %copy-done.57) | copy-start | bytes 1540
  110.5 4.9 %copy-start.11 = (bf16[128,768]{1,0:T(8,128)(2,1)S(1)}, bf16[128,768]{1,0:T(8,128)(2,1)}, u32[]{:S(2)}) copy-start(bf16[128,768]{1,0:T(8,128)(2,1)} %param.26) | copy-start | bytes 589828
  111.7 3.9 %copy-start.21 = (bf16[384,768]{1,0:T(8,128)(2,1)S(1)}, bf16[384,768]{1,0:T(8,128)(2,1)}, u32[]{:S(2)}) copy-start(bf16[384,768]{1,0:T(8,128)(2,1)} %param.30) | copy-start | bytes 1769476
  115.6 3.1 %copy-start.6 = (bf16[256,768]{0,1:T(8,128)(2,1)S(1)}, bf16[256,768]{0,1:T(8,128)(2,1)}, u32[]{:S(2)}) copy-start(bf16[256,768]{0,1:T(8,128)(2,1)} %copy-done.5) | copy-start | bytes 1179652
  126.3 3.1 %copy-start.45 = (f32[768]{0:T(1024)S(1)}, f32[768]{0:T(1024)}, u32[]{:S(2)}) copy-start(f32[768]{0:T(1024)} %get-tuple-element.50) | copy-start | bytes 9220
  126.3 3.1 %copy-start.34 = (f32[128,8]{0,1:T(8,128)S(1)}, f32[128,8]{0,1:T(8,128)}, u32[]{:S(2)}) copy-start(f32[128,8]{0,1:T(8,128)} %copy-done.32) | copy-start | bytes 12292
  126.3 3.1 %copy-start.44 = (f32[128]{0:T(128)S(1)}, f32[128]{0:T(128)}, u32[]{:S(2)}) copy-start(f32[128]{0:T(128)} %copy-done.42) | copy-start | bytes 1540
  126.3 3.1 %copy-start.50 = (s32[128]{0:T(128)S(1)}, s32[128]{0:T(128)}, u32[]{:S(2)}) copy-start(s32[128]{0:T(128)} %param.48) | copy-start | bytes 1540
  126.3 3.1 %copy-start.53 = (f32[128]{0:T(128)S(1)}, f32[128]{0:T(128)}, u32[]{:S(2)}) copy-start(f32[128]{0:T(128)} %copy-done.51) | copy-start | bytes 1540
  126.3 3.1 %copy-start.59 = (f32[128]{0:T(128)S(1)}, f32[128]{0:T(128)}, u32[]{:S(2)}) copy-start(f32[128]{0:T(128)} %copy-done.57) | copy-start | bytes 1540
  126.3 3.1 %copy-start.70 = (f32[128]{0:T(128)S(1)}, f32[128]{0:T(128)}, u32[]{:S(2)}) copy-start(f32[128]{0:T(128)} %copy-done.69) | copy-start | bytes 1540
  127.1 2.7 %collective-permute-start.5 = (bf16[128,1536]{1,0:T(8,128)(2,1)}, bf16[128,1536]{1,0:T(8,128)(2,1)}, u32[]{:S(2)}, u32[]{:S(2)}) collective-permute-start(bf16[128,1536]{1,0:T(8,128)(2,1)} %fusion.49), channel_id=1, source_target_pairs={{0,1},{1,0},{2,3},{3,2},{4,5},{5,4},{6,7},{7,6},{8,9},{9,8},{10,11... | collective-permute-start | bytes 1179656 | tf_op jit(solution)/shard_map/ppermute | solution.py:66
  129.5 2.1 %copy-start.15 = (bf16[384,2304]{1,0:T(8,128)(2,1)S(1)}, bf16[384,2304]{1,0:T(8,128)(2,1)}, u32[]{:S(2)}) copy-start(bf16[384,2304]{1,0:T(8,128)(2,1)} %copy-done.14) | copy-start | bytes 5308420
  132.9 42.1 %copy-start.8 = (f32[128,768]{1,0:T(8,128)S(1)}, f32[128,768]{1,0:T(8,128)}, u32[]{:S(2)}) copy-start(f32[128,768]{1,0:T(8,128)} %copy-done.7) | copy-start | bytes 1179652
  132.9 42.1 %copy-start.12 = (bf16[128,768]{1,0:T(8,128)(2,1)S(1)}, bf16[128,768]{1,0:T(8,128)(2,1)}, u32[]{:S(2)}) copy-start(bf16[128,768]{1,0:T(8,128)(2,1)} %param.26) | copy-start | bytes 589828
  132.9 42.1 %copy-start.68 = (f32[128]{0:T(128)S(1)}, f32[128]{0:T(128)}, u32[]{:S(2)}) copy-start(f32[128]{0:T(128)} %copy-done.67) | copy-start | bytes 1540
  174.6 2.0 %copy-start.31 = (bf16[768,8]{0,1:T(8,128)(2,1)S(1)}, bf16[768,8]{0,1:T(8,128)(2,1)}, u32[]{:S(2)}) copy-start(bf16[768,8]{0,1:T(8,128)(2,1)} %param.39) | copy-start | bytes 36868
  174.6 2.0 %copy-start.38 = (f32[768,8]{0,1:T(8,128)S(1)}, f32[768,8]{0,1:T(8,128)}, u32[]{:S(2)}) copy-start(f32[768,8]{0,1:T(8,128)} %param.41) | copy-start | bytes 73732
  174.6 2.0 %copy-start.39 = (f32[768,8]{0,1:T(8,128)S(1)}, f32[768,8]{0,1:T(8,128)}, u32[]{:S(2)}) copy-start(f32[768,8]{0,1:T(8,128)} %param.40) | copy-start | bytes 73732
  174.6 2.7 %copy-start.37 = (bf16[2,768]{1,0:T(2,128)(2,1)S(1)}, bf16[2,768]{1,0:T(2,128)(2,1)}, u32[]{:S(2)}) copy-start(bf16[2,768]{1,0:T(2,128)(2,1)} %param.42) | copy-start | bytes 9220
  174.6 2.7 %copy-start.62 = (f32[2,768]{1,0:T(2,128)S(1)}, f32[2,768]{1,0:T(2,128)}, u32[]{:S(2)}) copy-start(f32[2,768]{1,0:T(2,128)} %param.44) | copy-start | bytes 18436
  174.6 2.6 %copy-start.63 = (f32[2,768]{1,0:T(2,128)S(1)}, f32[2,768]{1,0:T(2,128)}, u32[]{:S(2)}) copy-start(f32[2,768]{1,0:T(2,128)} %param.43) | copy-start | bytes 18436
  174.7 3.3 %copy-start.47 = (bf16[32,12]{0,1:T(8,128)(2,1)S(1)}, bf16[32,12]{0,1:T(8,128)(2,1)}, u32[]{:S(2)}) copy-start(bf16[32,12]{0,1:T(8,128)(2,1)} %param.45) | copy-start | bytes 2308
  174.7 3.3 %copy-start.60 = (f32[32,12]{0,1:T(8,128)S(1)}, f32[32,12]{0,1:T(8,128)}, u32[]{:S(2)}) copy-start(f32[32,12]{0,1:T(8,128)} %param.47) | copy-start | bytes 4612
  174.7 3.2 %copy-start.61 = (f32[32,12]{0,1:T(8,128)S(1)}, f32[32,12]{0,1:T(8,128)}, u32[]{:S(2)}) copy-start(f32[32,12]{0,1:T(8,128)} %param.46) | copy-start | bytes 4612
  174.7 3.9 %copy-start.18 = (f32[1,1,24,2304]{3,1,2,0:T(1,128)S(1)}, f32[1,1,24,2304]{3,1,2,0:T(1,128)}, u32[]{:S(2)}) copy-start(f32[1,1,24,2304]{3,1,2,0:T(1,128)} %copy.106) | copy-start | bytes 663556
  174.7 3.9 %copy-start.27 = (f32[1,55296]{1,0:T(1,128)S(1)}, f32[1,55296]{1,0:T(1,128)}, u32[]{:S(2)}) copy-start(f32[1,55296]{1,0:T(1,128)} %param.29) | copy-start | bytes 663556
  174.7 3.8 %copy-start.28 = (f32[1,55296]{1,0:T(1,128)S(1)}, f32[1,55296]{1,0:T(1,128)}, u32[]{:S(2)}) copy-start(f32[1,55296]{1,0:T(1,128)} %param.28) | copy-start | bytes 663556
  175.1 5.9 %copy-start.26 = (f32[1,1,24,768]{3,1,2,0:T(1,128)S(1)}, f32[1,1,24,768]{3,1,2,0:T(1,128)}, u32[]{:S(2)}) copy-start(f32[1,1,24,768]{3,1,2,0:T(1,128)} %copy.108) | copy-start | bytes 221188
  175.1 5.9 %copy-start.35 = (f32[1,18432]{1,0:T(1,128)S(1)}, f32[1,18432]{1,0:T(1,128)}, u32[]{:S(2)}) copy-start(f32[1,18432]{1,0:T(1,128)} %param.32) | copy-start | bytes 221188
  175.1 5.8 %copy-start.36 = (f32[1,18432]{1,0:T(1,128)S(1)}, f32[1,18432]{1,0:T(1,128)}, u32[]{:S(2)}) copy-start(f32[1,18432]{1,0:T(1,128)} %param.31) | copy-start | bytes 221188
  (23 other events, 23.6 us)
